TPU v7x, 256 devices: a whole 4x4x8 slice. The times are simulated.
256 devices in a mesh: ctx: 8 (over z_lo, core), exp: 32 (over z_hi, x, y).
Axes of the slice: x: 4, y: 4, z: 8 (z_hi: 2, z_lo: 4; z = z_hi * 4 + z_lo), core: 2. Of those that a mesh axis runs over, the one named last changes fastest.
Arguments:
- queries: bfloat16 [1024, 12288], P('ctx', 'exp'), may hold values from -160 to 160
- latents: bfloat16 [1024, 512], P('ctx'), may hold values from -6 to 6
- rotary_keys: bfloat16 [1024, 64], P('ctx'), may hold values from -5 to 5
- block_order: int32 [8], replicated, may hold values from 0 to 7, each once
- absorb_key: bfloat16 [64, 128, 512], P('exp'), may hold values from -0.5 to 0.5
- absorb_value: bfloat16 [64, 512, 128], P('exp'), may hold values from -0.25 to 0.25
- output_weight: bfloat16 [8192, 7168], P('exp', 'ctx'), may hold values from -0.0625 to 0.0625
- residual: bfloat16 [1024, 7168], P(('ctx', 'exp')), may hold values from -6 to 6
- norm_gain: bfloat16 [7168], replicated, may hold values from 0.25 to 1.75
- route_experts: int32 [1024, 8], replicated, may hold values from 0 to 31, all different within a row; in each aligned block of 128 rows (0 to 127, 128 to 255, ...) at most 40 rows name the same one
- route_weights: float32 [1024, 8], replicated, may hold values from 0.1 to 0.6
- gate_weight: bfloat16 [7168, 65536], P(None, ('ctx', 'exp')), may hold values from -0.0625 to 0.0625
- up_weight: bfloat16 [7168, 65536], P(None, ('ctx', 'exp')), may hold values from -0.0625 to 0.0625
- down_weight: bfloat16 [65536, 7168], P(('ctx', 'exp')), may hold values from -0.125 to 0.125
Outputs:
- block_output: float32 [1024, 7168], P(('ctx', 'exp'))
Inputs may be any that keep to these rules, and one draw needn't show every extreme that they name: `route_experts`: within each context block (aligned blocks of 128 rows) no expert is named by more than 40 rows, a bound that some block reaches. `block_order`: each block number appears once.
All inputs are finite; a program needn't handle non-finite values.
Results may differ from a plain program's by a relative error of at most 0.019.
Values may be sent and summed in bfloat16 or wider, within the bound.
No kernel may reach another device: no remote copies, remote signals or barrier semaphores. Data moves between devices by JAX's collectives and lax.ppermute only.
A program may use at most 128 MiB of HBM per device.

v0:
```python
import math

import jax
import jax.numpy as jnp
from jax import lax
from jax.sharding import Mesh, PartitionSpec as P

FF = 2048
CAPACITY = 40
EPSILON = 1e-06

CTX = ("zl", "core")
EXP = ("zh", "x2", "x1", "y")
PATCH = ("x1", "y")
PLANE = ("x2", "x1", "y")
SIZES = (4, 2, 2, 2, 2, 4)


def all_to_all(value, axes):
    return lax.all_to_all(value, axes, split_axis=0, concat_axis=0, tiled=True)


def swap(value, axes, count, mask):
    return lax.ppermute(value, axes, [(i, i ^ mask) for i in range(count)])


def gather_context(value):
    planes = [value] + [swap(value, "zl", 4, mask) for mask in range(1, 4)]
    mine = jnp.stack(planes)
    return jnp.concatenate([mine, swap(mine, "core", 2, 1)])


def sources(here):
    return here ^ jnp.array([0, 2, 4, 6, 1, 3, 5, 7], jnp.int32)


def slots(experts, owners, position):
    matches = experts[:, None, :] == owners[None, :, None]
    chosen = jnp.any(matches, axis=2)
    before = jnp.dot(
        (position[None, :] < position[:, None]).astype(jnp.bfloat16),
        chosen.astype(jnp.bfloat16),
        preferred_element_type=jnp.float32,
    ).astype(jnp.int32)
    columns = jnp.arange(CAPACITY, dtype=jnp.int32)
    return matches, chosen[:, :, None] & (before[:, :, None] == columns)


def attend(queries, latents, rotary_keys, block_order, absorb_key, absorb_value):
    block_size = queries.shape[0]
    head_count, plain_width, latent_width = absorb_key.shape
    rotary_width = rotary_keys.shape[1]
    score_scale = 1.0 / math.sqrt(plain_width + rotary_width)
    keys = gather_context(jnp.concatenate([latents, rotary_keys], axis=1)).reshape(
        8 * block_size, latent_width + rotary_width
    )
    ordered = jnp.arange(block_size, dtype=jnp.int32).reshape(2, 16, 4).transpose(1, 0, 2).reshape(-1)
    shaped = queries.reshape(2, 16, 4, head_count, plain_width + rotary_width)
    shaped = shaped.transpose(1, 0, 2, 3, 4).reshape(
        block_size, head_count, plain_width + rotary_width
    )
    here = lax.axis_index(CTX)
    source_blocks = sources(here)
    source_order = jnp.sum(
        jnp.where(
            jnp.arange(8, dtype=jnp.int32)[None, :] == source_blocks[:, None],
            block_order[None, :],
            0,
        ),
        axis=1,
    )
    row_pos = jnp.tile(source_order[0] * block_size + ordered, head_count)
    key_pos = (
        source_order[:, None] * block_size + jnp.arange(block_size, dtype=jnp.int32)[None, :]
    ).reshape(-1)
    query_latent = jnp.einsum(
        "thn,hnl->htl", shaped[:, :, :plain_width], absorb_key, preferred_element_type=jnp.float32
    ).astype(jnp.bfloat16)
    query = jnp.concatenate(
        [query_latent, shaped[:, :, plain_width:].transpose(1, 0, 2)], axis=2
    ).reshape(head_count * block_size, latent_width + rotary_width)
    scores = (
        jnp.einsum("rl,nl->rn", query, keys, preferred_element_type=jnp.float32) * score_scale
    )
    visible = key_pos[None, :] <= row_pos[:, None]
    scores = jnp.where(visible, scores, -1e30)
    row_max = jnp.max(scores, axis=1, keepdims=True)
    exponent = jnp.where(visible, jnp.exp(scores - row_max), 0.0)
    row_sum = jnp.sum(exponent, axis=1, keepdims=True)
    weighted = jnp.dot(
        exponent.astype(jnp.bfloat16),
        keys[:, :latent_width],
        preferred_element_type=jnp.float32,
    )
    out_latent = (
        (weighted / row_sum).astype(jnp.bfloat16).reshape(head_count, block_size, latent_width)
    )
    return (
        jnp.einsum("htl,hlv->thv", out_latent, absorb_value, preferred_element_type=jnp.float32)
        .astype(jnp.bfloat16)
        .reshape(block_size, -1)
    )


def on_device(
    queries,
    latents,
    rotary_keys,
    block_order,
    absorb_key,
    absorb_value,
    output_weight,
    residual,
    norm_gain,
    route_experts,
    route_weights,
    gate_weight,
    up_weight,
    down_weight,
):
    block_size = queries.shape[0]
    width = norm_gain.shape[0]
    share = output_weight.shape[1]
    hidden_share = gate_weight.shape[1]
    own_tokens = residual.shape[0]
    here = lax.axis_index(CTX)
    member = lax.axis_index(EXP)
    patch_here = lax.axis_index(PATCH)

    early = hidden_share * 9 // 16
    down_early = all_to_all(
        down_weight[:early].reshape(early, 8, share).transpose(1, 0, 2), PATCH
    )

    owners = (here ^ jnp.arange(8, dtype=jnp.int32)) * 4 + member * hidden_share // FF
    own_experts = lax.dynamic_slice_in_dim(route_experts, here * block_size, block_size, 0)
    own_weights = lax.dynamic_slice_in_dim(route_weights, here * block_size, block_size, 0)
    row = jnp.arange(block_size, dtype=jnp.int32)
    arrival = row % 4 + row // 4 % 2 * 64 + row // 8 % 8 * 4 + row // 64 * 32
    arrival_experts = own_experts.reshape(2, 2, 8, 4, -1).transpose(1, 2, 0, 3, 4)
    arrival_experts = arrival_experts.reshape(own_experts.shape)
    arranged = slots(arrival_experts, owners, arrival)[1].astype(jnp.bfloat16)
    matches, selected = slots(own_experts, owners, row)
    gate_share = jnp.sum(jnp.where(matches, own_weights[:, None, :], 0.0), axis=2)
    weighing = jnp.where(selected, gate_share[:, :, None], 0.0).astype(jnp.bfloat16)
    weighing = weighing.reshape(block_size, 8 * CAPACITY)

    head_values = attend(queries, latents, rotary_keys, block_order, absorb_key, absorb_value)
    gathered = gather_context(head_values)
    gathered = (
        gathered.reshape(8, 16, 8, -1).transpose(1, 0, 2, 3).reshape(8 * block_size, -1)
    )
    projected = jnp.dot(gathered, output_weight, preferred_element_type=jnp.float32).astype(
        jnp.bfloat16
    )
    projected, down_early, residual_here = lax.optimization_barrier(
        (projected, down_early, residual)
    )
    residual_beside = swap(residual_here, "zh", 2, 1)
    landed = all_to_all(projected.reshape(16, 64, share), PLANE)
    late_rows = down_weight[early:].reshape(hidden_share - early, 8, share).transpose(1, 0, 2)
    landed, late_rows, arranged, weighing, residual_beside = lax.optimization_barrier(
        (landed, late_rows, arranged, weighing, residual_beside)
    )
    partial = jnp.sum(landed.astype(jnp.float32), axis=0).astype(jnp.bfloat16)
    partial = partial.reshape(2, 4, 2 * own_tokens, share)
    pieces = jnp.stack([partial[0], swap(partial[1], "core", 2, 1)], axis=1)
    pieces = pieces.reshape(2, 2, 2, 2 * own_tokens, share)
    for axis, bit in ((0, 4), (1, 2)):
        pieces = jnp.where((here & bit) > 0, jnp.flip(pieces, axis), pieces)
    pieces = jnp.broadcast_to(
        pieces.reshape(4, 1, 2, 2 * own_tokens, share), (4, 2, 2, 2 * own_tokens, share)
    ).reshape(8, 2, 2 * own_tokens, share)
    pieces = all_to_all(pieces, ("zl", "zh")).reshape(4, 2, 2, 2 * own_tokens, share)
    summed = pieces[:, 0].astype(jnp.float32) + pieces[:, 1].astype(jnp.float32)
    summed = jnp.where((here & 1) > 0, jnp.flip(summed, 1), summed)
    rows = summed.transpose(2, 0, 1, 3).reshape(2 * own_tokens, width)
    half = lax.axis_index("zh")
    both_residuals = jnp.concatenate(
        [
            jnp.where(half > 0, residual_beside, residual),
            jnp.where(half > 0, residual, residual_beside),
        ]
    )
    both_sums = rows + both_residuals.astype(jnp.float32)
    residual_sum = lax.dynamic_slice_in_dim(both_sums, half * own_tokens, own_tokens, 0)
    normed = (
        both_sums
        * lax.rsqrt(jnp.mean(both_sums * both_sums, axis=1, keepdims=True) + EPSILON)
        * norm_gain.astype(jnp.float32)
    ).astype(jnp.bfloat16)

    columns = normed.reshape(2 * own_tokens, 8, share).transpose(1, 0, 2)
    spread = jnp.broadcast_to(columns[None], (2,) + columns.shape)
    block_columns = all_to_all(
        spread.reshape(16, 2 * own_tokens, share), PLANE
    ).reshape(block_size, share)

    outgoing = jnp.einsum(
        "trc,td->rcd",
        arranged,
        block_columns,
        preferred_element_type=jnp.float32,
    ).astype(jnp.bfloat16)
    outgoing, late_rows = lax.optimization_barrier((outgoing, late_rows))
    down_late = all_to_all(late_rows, PATCH)
    outgoing = outgoing.reshape(4, 2, CAPACITY, share)
    by_plane = jnp.stack([outgoing[:, 0], swap(outgoing[:, 1], "core", 2, 1)], axis=1)
    by_plane = [by_plane[0]] + [swap(by_plane[mask], "zl", 4, mask) for mask in range(1, 4)]
    arrived = jnp.concatenate(by_plane).reshape(8 * CAPACITY, share)
    arrived, down_late = lax.optimization_barrier((arrived, down_late))
    down_columns = jnp.concatenate([down_early, down_late], axis=1).reshape(-1, share)

    split = 192
    beside_all = swap(arrived, "x1", 2, 1)
    first_pieces = [arrived[:split]] + [swap(arrived[:split], "y", 4, mask) for mask in range(1, 4)]
    first_pieces = (
        first_pieces
        + [beside_all[:split]]
        + [swap(piece, "x1", 2, 1) for piece in first_pieces[1:]]
    )
    pair = jnp.stack([arrived[split:], beside_all[split:]])
    pairs = [pair] + [swap(pair, "y", 4, mask) for mask in range(1, 4)]
    last_pieces = [both[0] for both in pairs] + [both[1] for both in pairs]

    weights = []
    for mask in range(8):
        first = (patch_here ^ mask) * share
        weights.append(
            jnp.concatenate(
                [
                    lax.dynamic_slice_in_dim(gate_weight, first, share, 0),
                    lax.dynamic_slice_in_dim(up_weight, first, share, 0),
                ],
                axis=1,
            )
        )

    def activate(pieces):
        pre = 0.0
        for piece, weight in zip(pieces, weights):
            pre = pre + jnp.dot(piece, weight, preferred_element_type=jnp.float32)
        return (jax.nn.silu(pre[:, :hidden_share]) * pre[:, hidden_share:]).astype(jnp.bfloat16)

    activated = jnp.concatenate([activate(first_pieces), activate(last_pieces)])
    hidden = all_to_all(
        jnp.broadcast_to(activated[None], (8,) + activated.shape), PATCH
    ).transpose(1, 0, 2)
    computed = jnp.dot(
        hidden.reshape(8 * CAPACITY, 8 * hidden_share),
        down_columns,
        preferred_element_type=jnp.float32,
    )
    back = computed.astype(jnp.bfloat16).reshape(4, 2, CAPACITY, share)
    back = jnp.stack([back[0]] + [swap(back[mask], "zl", 4, mask) for mask in range(1, 4)])
    returned = jnp.stack([back[:, 0], swap(back[:, 1], "core", 2, 1)], axis=1)
    block_total = jnp.dot(
        weighing, returned.reshape(8 * CAPACITY, share), preferred_element_type=jnp.float32
    ).astype(jnp.bfloat16)
    parts = all_to_all(block_total.reshape(32, own_tokens, share), EXP)
    expert_total = (
        jnp.sum(parts.reshape(4, 8, own_tokens, share).astype(jnp.float32), axis=0)
        .transpose(1, 0, 2)
        .reshape(own_tokens, width)
    )
    return residual_sum + expert_total


def solution(mesh):
    finer = Mesh(mesh.devices.reshape(SIZES), CTX + EXP)
    return jax.shard_map(
        on_device,
        mesh=finer,
        in_specs=(
            P(CTX, EXP),
            P(CTX, None),
            P(CTX, None),
            P(),
            P(EXP, None, None),
            P(EXP, None, None),
            P(EXP, CTX),
            P(CTX + EXP, None),
            P(),
            P(),
            P(),
            P(None, CTX + EXP),
            P(None, CTX + EXP),
            P(CTX + EXP, None),
        ),
        out_specs=P(CTX + EXP, None),
        check_vma=False,
    )
```

profile of v0, /device:TPU:32, one launch (start us, length us, event | category | flops | bytes accessed | tf_op | source)
XLA Modules:
  0.0 233.7 jit_solution(9899604788861007619)
XLA Ops:
  1.8 3.4 %collective-permute-start.1 = (bf16[128,576]{0,1:T(8,128)(2,1)S(1)}, bf16[128,576]{0,1:T(8,128)(2,1)S(1)}, u32[]{:S(2)}, u32[]{:S(2)}) collective-permute-start(bf16[128,576]{0,1:T(8,128)(2,1)S(1)} %get-tuple-element.62), channel_id=1, source_target_pairs={{0,128},{64,192},{128,0},{192,64},{1,129},{65,193},{129,1},{193,65... | collective-permute-start | bytes 442376 | tf_op jit(solution)/shard_map/ppermute | solution.py:24
  8.3 5.5 %all-to-all-start = ((bf16[8,144,896]{2,1,0:T(8,128)(2,1)}), bf16[8,144,896]{2,1,0:T(8,128)(2,1)S(1)}, u32[]{:S(2)}, u32[]{:S(2)}) async-start(bf16[8,144,896]{2,1,0:T(8,128)(2,1)} %bitcast.202), calls=%async_computation | async-start | bytes 4128768 | tf_op jit(solution)/shard_map/all_to_all | solution.py:20
  17.7 1.9 collective-permute-done.3
  22.3 3.9 %collective-permute-start.5 = (bf16[128,256]{1,0:T(8,128)(2,1)S(1)}, bf16[128,256]{1,0:T(8,128)(2,1)S(1)}, u32[]{:S(2)}, u32[]{:S(2)}) collective-permute-start(bf16[128,256]{1,0:T(8,128)(2,1)S(1)} %copy.108), channel_id=1, source_target_pairs={{0,128},{64,192},{128,0},{192,64},{1,129},{65,193},{129,1},{193,65... | collective-permute-start | bytes 196616 | tf_op jit(solution)/shard_map/ppermute | solution.py:24
  26.6 3.8 %collective-permute-done.5 = bf16[128,256]{1,0:T(8,128)(2,1)S(1)} collective-permute-done((bf16[128,256]{1,0:T(8,128)(2,1)S(1)}, bf16[128,256]{1,0:T(8,128)(2,1)S(1)}, u32[]{:S(2)}, u32[]{:S(2)}) %collective-permute-start.5) | collective-permute-done | bytes 65568 | tf_op jit(solution)/shard_map/ppermute | solution.py:24
  34.0 2.0 convolution_convert_fusion
  35.9 3.0 %all-to-all-done = bf16[8,144,896]{2,1,0:T(8,128)(2,1)S(1)} async-done(((bf16[8,144,896]{2,1,0:T(8,128)(2,1)}), bf16[8,144,896]{2,1,0:T(8,128)(2,1)S(1)}, u32[]{:S(2)}, u32[]{:S(2)}) %all-to-all-start) | async-done | bytes 2064416 | tf_op jit(solution)/shard_map/all_to_all | solution.py:20
  40.3 5.5 %all-to-all-start.1 = ((bf16[16,64,896]{2,1,0:T(8,128)(2,1)}), bf16[16,64,896]{2,1,0:T(8,128)(2,1)}, u32[]{:S(2)}, u32[]{:S(2)}) async-start(bf16[16,64,896]{2,1,0:T(8,128)(2,1)} %bitcast.27), calls=%async_computation.1 | async-start | bytes 3670016 | tf_op jit(solution)/shard_map/all_to_all | solution.py:20
  49.8 5.6 %collective-permute-start.8 = (bf16[4,7168]{1,0:T(4,128)(2,1)S(1)}, bf16[4,7168]{1,0:T(4,128)(2,1)S(1)}, u32[]{:S(2)}, u32[]{:S(2)}) collective-permute-start(bf16[4,7168]{1,0:T(4,128)(2,1)S(1)} %copy-done.17), channel_id=1, source_target_pairs={{0,16},{16,0},{1,17},{17,1},{2,18},{18,2},{3,19},{19,3},{4,20},{20... | collective-permute-start | bytes 172040 | tf_op jit(solution)/shard_map/ppermute | solution.py:24
  55.6 2.4 %collective-permute-done.8 = bf16[4,7168]{1,0:T(4,128)(2,1)S(1)} collective-permute-done((bf16[4,7168]{1,0:T(4,128)(2,1)S(1)}, bf16[4,7168]{1,0:T(4,128)(2,1)S(1)}, u32[]{:S(2)}, u32[]{:S(2)}) %collective-permute-start.8) | collective-permute-done | bytes 57376 | tf_op jit(solution)/shard_map/ppermute | solution.py:24
  58.0 14.3 %all-to-all-done.1 = bf16[16,64,896]{2,1,0:T(8,128)(2,1)} async-done(((bf16[16,64,896]{2,1,0:T(8,128)(2,1)}), bf16[16,64,896]{2,1,0:T(8,128)(2,1)}, u32[]{:S(2)}, u32[]{:S(2)}) %all-to-all-start.1) | async-done | bytes 1835040 | tf_op jit(solution)/shard_map/all_to_all | solution.py:20
  76.2 7.4 %all-to-all-start.2 = ((bf16[8,2,8,896]{3,2,1,0:T(8,128)(2,1)}), bf16[8,2,8,896]{3,2,1,0:T(8,128)(2,1)S(1)}, u32[]{:S(2)}, u32[]{:S(2)}) async-start(bf16[8,2,8,896]{3,2,1,0:T(8,128)(2,1)} %bitcast.39), calls=%async_computation.2 | async-start | bytes 458752 | tf_op jit(solution)/shard_map/all_to_all | solution.py:20
  83.7 9.7 %all-to-all-done.2 = bf16[8,2,8,896]{3,2,1,0:T(8,128)(2,1)S(1)} async-done(((bf16[8,2,8,896]{3,2,1,0:T(8,128)(2,1)}), bf16[8,2,8,896]{3,2,1,0:T(8,128)(2,1)S(1)}, u32[]{:S(2)}, u32[]{:S(2)}) %all-to-all-start.2) | async-done | bytes 229408 | tf_op jit(solution)/shard_map/all_to_all | solution.py:20
  93.8 12.1 %all_to_all.35 = bf16[16,8,896]{2,1,0:T(8,128)(2,1)S(1)} all-to-all(bf16[16,8,896]{2,1,0:T(8,128)(2,1)S(1)} %bitcast.227), channel_id=1, replica_groups=mesh['zl'=4,'core'=2,'zh'=2,'x2'=2,'x1'=2,'y'=4] {'x2','x1','y'}, dimensions={0} | all-to-all | bytes 458752 | tf_op jit(solution)/shard_map/all_to_all | solution.py:20
  106.2 4.3 %all-to-all-start.4 = ((bf16[8,112,896]{2,1,0:T(8,128)(2,1)}), bf16[8,112,896]{2,1,0:T(8,128)(2,1)}, u32[]{:S(2)}, u32[]{:S(2)}) async-start(bf16[8,112,896]{2,1,0:T(8,128)(2,1)} %bitcast.204), calls=%async_computation.4 | async-start | bytes 3211264 | tf_op jit(solution)/shard_map/all_to_all | solution.py:20
  112.6 2.2 collective-permute-start.12
  116.1 5.5 %constant_dynamic-slice_fusion.10 = (bf16[896,256]{1,0:T(8,128)(2,1)S(1)}, bf16[896,256]{1,0:T(8,128)(2,1)S(1)}, bf16[896,256]{1,0:T(8,128)(2,1)}, bf16[896,256]...) fusion(bf16[7168,256]{1,0:T(8,128)(2,1)} %param.27, ...), kind=kLoop, calls=%fused_computation.164 | loop fusion | bytes 14680096 | tf_op jit(solution)/shard_map/dynamic_slice | solution.py:233
  121.6 3.5 %collective-permute-done.12 = bf16[2,40,896]{2,1,0:T(8,128)(2,1)S(1)} collective-permute-done((bf16[2,40,896]{2,1,0:T(8,128)(2,1)S(1)}, bf16[2,40,896]{2,1,0:T(8,128)(2,1)S(1)}, u32[]{:S(2)}, u32[]{:S(2)}) %collective-permute-start.12) | collective-permute-done | bytes 143392 | tf_op jit(solution)/shard_map/ppermute | solution.py:24
  125.2 3.7 %collective-permute-done.13 = bf16[2,40,896]{2,1,0:T(8,128)(2,1)S(1)} collective-permute-done((bf16[2,40,896]{2,1,0:T(8,128)(2,1)S(1)}, bf16[2,40,896]{2,1,0:T(8,128)(2,1)S(1)}, u32[]{:S(2)}, u32[]{:S(2)}) %collective-permute-start.13) | collective-permute-done | bytes 143392 | tf_op jit(solution)/shard_map/ppermute | solution.py:24
  138.2 10.0 %collective-permute-done.15 = bf16[192,896]{1,0:T(8,128)(2,1)S(1)} collective-permute-done((bf16[192,896]{1,0:T(8,128)(2,1)S(1)}, bf16[192,896]{1,0:T(8,128)(2,1)S(1)}, u32[]{:S(2)}, u32[]{:S(2)}) %collective-permute-start.15) | collective-permute-done | bytes 344096 | tf_op jit(solution)/shard_map/ppermute | solution.py:24
  148.2 2.2 collective-permute-start.19
  153.5 2.0 collective-permute-start.23
  156.6 2.8 %collective-permute-done.19 = bf16[192,896]{1,0:T(8,128)(2,1)S(1)} collective-permute-done((bf16[192,896]{1,0:T(8,128)(2,1)S(1)}, bf16[192,896]{1,0:T(8,128)(2,1)S(1)}, u32[]{:S(2)}, u32[]{:S(2)}) %collective-permute-start.19) | collective-permute-done | bytes 344096 | tf_op jit(solution)/shard_map/ppermute | solution.py:24
  161.3 5.5 %collective-permute-done.20 = bf16[192,896]{1,0:T(8,128)(2,1)S(1)} collective-permute-done((bf16[192,896]{1,0:T(8,128)(2,1)S(1)}, bf16[192,896]{1,0:T(8,128)(2,1)S(1)}, u32[]{:S(2)}, u32[]{:S(2)}) %collective-permute-start.20) | collective-permute-done | bytes 344096 | tf_op jit(solution)/shard_map/ppermute | solution.py:24
  167.2 5.1 %collective-permute-done.18 = bf16[192,896]{1,0:T(8,128)(2,1)S(1)} collective-permute-done((bf16[192,896]{1,0:T(8,128)(2,1)S(1)}, bf16[192,896]{1,0:T(8,128)(2,1)S(1)}, u32[]{:S(2)}, u32[]{:S(2)}) %collective-permute-start.18) | collective-permute-done | bytes 344096 | tf_op jit(solution)/shard_map/ppermute | solution.py:24
  172.8 2.3 collective-permute-done.23
  177.2 18.6 %all_to_all.36 = bf16[8,320,256]{2,1,0:T(8,128)(2,1)S(1)} all-to-all(bf16[8,320,256]{2,1,0:T(8,128)(2,1)S(1)} %broadcast_in_dim.100), channel_id=1, replica_groups=mesh['zl'=4,'core'=2,'zh'=2,'x2'=2,'x1'=2,'y'=4] {'x1','y'}, dimensions={0} | all-to-all | bytes 2621440 | tf_op jit(solution)/shard_map/all_to_all | solution.py:20
  195.8 2.9 %fusion.8 = bf16[320,896]{1,0:T(8,128)(2,1)S(1)} fusion(bf16[8,112,896]{2,1,0:T(8,128)(2,1)} %all-to-all-done.4, bf16[8,144,896]{2,1,0:T(8,128)(2,1)S(1)} %copy-done.2, bf16[8,320,256]{2,1,0:T(8,128)(2,1)S(1)} %all_to_all.36), kind=kOutput, calls=%fused_computation.11 | convolution fusion | flops 1182031872 | bytes 5554176 | tf_op jit(solution)/shard_map/dot_general | solution.py:249
  199.0 3.4 %collective-permute-start.26 = (bf16[2,40,896]{2,1,0:T(8,128)(2,1)S(1)}, bf16[2,40,896]{2,1,0:T(8,128)(2,1)S(1)}, u32[]{:S(2)}, u32[]{:S(2)}) collective-permute-start(bf16[2,40,896]{2,1,0:T(8,128)(2,1)S(1)} %bitcast.249), channel_id=1, source_target_pairs={{0,192},{64,128},{128,64},{192,0},{1,193},{65,129},{129,65},{193,1... | collective-permute-start | bytes 430088 | tf_op jit(solution)/shard_map/ppermute | solution.py:24
  205.1 4.8 %collective-permute-done.26 = bf16[2,40,896]{2,1,0:T(8,128)(2,1)S(1)} collective-permute-done((bf16[2,40,896]{2,1,0:T(8,128)(2,1)S(1)}, bf16[2,40,896]{2,1,0:T(8,128)(2,1)S(1)}, u32[]{:S(2)}, u32[]{:S(2)}) %collective-permute-start.26) | collective-permute-done | bytes 143392 | tf_op jit(solution)/shard_map/ppermute | solution.py:24
  212.8 4.6 %all-to-all-start.6 = ((bf16[32,4,896]{2,1,0:T(4,128)(2,1)}), bf16[32,4,896]{2,1,0:T(4,128)(2,1)S(1)}, u32[]{:S(2)}, u32[]{:S(2)}) async-start(bf16[32,4,896]{2,1,0:T(4,128)(2,1)} %reshape.377), calls=%async_computation.6 | async-start | bytes 458752 | tf_op jit(solution)/shard_map/all_to_all | solution.py:20
  217.4 15.4 %all-to-all-done.6 = bf16[32,4,896]{2,1,0:T(4,128)(2,1)S(1)} async-done(((bf16[32,4,896]{2,1,0:T(4,128)(2,1)}), bf16[32,4,896]{2,1,0:T(4,128)(2,1)S(1)}, u32[]{:S(2)}, u32[]{:S(2)}) %all-to-all-start.6) | async-done | bytes 229408 | tf_op jit(solution)/shard_map/all_to_all | solution.py:20
  (188 shorter events, 53.2 us)
Async XLA Ops:
  1.8 14.9 %collective-permute-start.1 = (bf16[128,576]{0,1:T(8,128)(2,1)S(1)}, bf16[128,576]{0,1:T(8,128)(2,1)S(1)}, u32[]{:S(2)}, u32[]{:S(2)}) collective-permute-start(bf16[128,576]{0,1:T(8,128)(2,1)S(1)} %get-tuple-element.62), channel_id=1, source_target_pairs={{0,128},{64,192},{128,0},{192,64},{1,129},{65,193},{129,1},{193,65... | collective-permute-start | bytes 442376 | tf_op jit(solution)/shard_map/ppermute | solution.py:24
  5.2 12.2 %collective-permute-start.2 = (bf16[128,576]{0,1:T(8,128)(2,1)S(1)}, bf16[128,576]{0,1:T(8,128)(2,1)S(1)}, u32[]{:S(2)}, u32[]{:S(2)}) collective-permute-start(bf16[128,576]{0,1:T(8,128)(2,1)S(1)} %get-tuple-element.62), channel_id=1, source_target_pairs={{0,192},{64,128},{128,64},{192,0},{1,193},{65,129},{129,65},{193,1... | collective-permute-start | bytes 442376 | tf_op jit(solution)/shard_map/ppermute | solution.py:24
  5.2 12.1 %collective-permute-start = (bf16[128,576]{0,1:T(8,128)(2,1)S(1)}, bf16[128,576]{0,1:T(8,128)(2,1)S(1)}, u32[]{:S(2)}, u32[]{:S(2)}) collective-permute-start(bf16[128,576]{0,1:T(8,128)(2,1)S(1)} %get-tuple-element.62), channel_id=1, source_target_pairs={{0,64},{64,0},{128,192},{192,128},{1,65},{65,1},{129,193},{193,129... | collective-permute-start | bytes 442376 | tf_op jit(solution)/shard_map/ppermute | solution.py:24
  8.3 30.7 %all-to-all-start = ((bf16[8,144,896]{2,1,0:T(8,128)(2,1)}), bf16[8,144,896]{2,1,0:T(8,128)(2,1)S(1)}, u32[]{:S(2)}, u32[]{:S(2)}) async-start(bf16[8,144,896]{2,1,0:T(8,128)(2,1)} %bitcast.202), calls=%async_computation | async-start | bytes 4128768 | tf_op jit(solution)/shard_map/all_to_all | solution.py:20
  17.5 2.1 collective-permute-start.3
  22.2 4.4 %collective-permute-start.4 = (bf16[128,256]{1,0:T(8,128)(2,1)S(1)}, bf16[128,256]{1,0:T(8,128)(2,1)S(1)}, u32[]{:S(2)}, u32[]{:S(2)}) collective-permute-start(bf16[128,256]{1,0:T(8,128)(2,1)S(1)} %copy.108), channel_id=1, source_target_pairs={{0,64},{64,0},{128,192},{192,128},{1,65},{65,1},{129,193},{193,129... | collective-permute-start | bytes 196616 | tf_op jit(solution)/shard_map/ppermute | solution.py:24
  22.3 8.1 %collective-permute-start.5 = (bf16[128,256]{1,0:T(8,128)(2,1)S(1)}, bf16[128,256]{1,0:T(8,128)(2,1)S(1)}, u32[]{:S(2)}, u32[]{:S(2)}) collective-permute-start(bf16[128,256]{1,0:T(8,128)(2,1)S(1)} %copy.108), channel_id=1, source_target_pairs={{0,128},{64,192},{128,0},{192,64},{1,129},{65,193},{129,1},{193,65... | collective-permute-start | bytes 196616 | tf_op jit(solution)/shard_map/ppermute | solution.py:24
  26.2 6.0 %collective-permute-start.6 = (bf16[128,256]{1,0:T(8,128)(2,1)S(1)}, bf16[128,256]{1,0:T(8,128)(2,1)S(1)}, u32[]{:S(2)}, u32[]{:S(2)}) collective-permute-start(bf16[128,256]{1,0:T(8,128)(2,1)S(1)} %copy.108), channel_id=1, source_target_pairs={{0,192},{64,128},{128,64},{192,0},{1,193},{65,129},{129,65},{193,1... | collective-permute-start | bytes 196616 | tf_op jit(solution)/shard_map/ppermute | solution.py:24
  32.3 1.6 collective-permute-start.7
  40.3 32.1 %all-to-all-start.1 = ((bf16[16,64,896]{2,1,0:T(8,128)(2,1)}), bf16[16,64,896]{2,1,0:T(8,128)(2,1)}, u32[]{:S(2)}, u32[]{:S(2)}) async-start(bf16[16,64,896]{2,1,0:T(8,128)(2,1)} %bitcast.27), calls=%async_computation.1 | async-start | bytes 3670016 | tf_op jit(solution)/shard_map/all_to_all | solution.py:20
  49.8 8.2 %collective-permute-start.8 = (bf16[4,7168]{1,0:T(4,128)(2,1)S(1)}, bf16[4,7168]{1,0:T(4,128)(2,1)S(1)}, u32[]{:S(2)}, u32[]{:S(2)}) collective-permute-start(bf16[4,7168]{1,0:T(4,128)(2,1)S(1)} %copy-done.17), channel_id=1, source_target_pairs={{0,16},{16,0},{1,17},{17,1},{2,18},{18,2},{3,19},{19,3},{4,20},{20... | collective-permute-start | bytes 172040 | tf_op jit(solution)/shard_map/ppermute | solution.py:24
  76.2 17.2 %all-to-all-start.2 = ((bf16[8,2,8,896]{3,2,1,0:T(8,128)(2,1)}), bf16[8,2,8,896]{3,2,1,0:T(8,128)(2,1)S(1)}, u32[]{:S(2)}, u32[]{:S(2)}) async-start(bf16[8,2,8,896]{3,2,1,0:T(8,128)(2,1)} %bitcast.39), calls=%async_computation.2 | async-start | bytes 458752 | tf_op jit(solution)/shard_map/all_to_all | solution.py:20
  106.2 24.3 %all-to-all-start.4 = ((bf16[8,112,896]{2,1,0:T(8,128)(2,1)}), bf16[8,112,896]{2,1,0:T(8,128)(2,1)}, u32[]{:S(2)}, u32[]{:S(2)}) async-start(bf16[8,112,896]{2,1,0:T(8,128)(2,1)} %bitcast.204), calls=%async_computation.4 | async-start | bytes 3211264 | tf_op jit(solution)/shard_map/all_to_all | solution.py:20
  110.6 1.8 collective-permute-start.10
  112.5 9.1 %collective-permute-start.11 = (bf16[2,40,896]{2,1,0:T(8,128)(2,1)S(1)}, bf16[2,40,896]{2,1,0:T(8,128)(2,1)S(1)}, u32[]{:S(2)}, u32[]{:S(2)}) collective-permute-start(bf16[2,40,896]{2,1,0:T(8,128)(2,1)S(1)} %get-tuple-element.56), channel_id=1, source_target_pairs={{0,64},{64,0},{128,192},{192,128},{1,65},{65,1},{129,193},{193,129... | collective-permute-start | bytes 430088 | tf_op jit(solution)/shard_map/ppermute | solution.py:24
  112.6 12.5 %collective-permute-start.12 = (bf16[2,40,896]{2,1,0:T(8,128)(2,1)S(1)}, bf16[2,40,896]{2,1,0:T(8,128)(2,1)S(1)}, u32[]{:S(2)}, u32[]{:S(2)}) collective-permute-start(bf16[2,40,896]{2,1,0:T(8,128)(2,1)S(1)} %get-tuple-element.58), channel_id=1, source_target_pairs={{0,128},{64,192},{128,0},{192,64},{1,129},{65,193},{129,1},{193,65... | collective-permute-start | bytes 430088 | tf_op jit(solution)/shard_map/ppermute | solution.py:24
  114.9 14.0 %collective-permute-start.13 = (bf16[2,40,896]{2,1,0:T(8,128)(2,1)S(1)}, bf16[2,40,896]{2,1,0:T(8,128)(2,1)S(1)}, u32[]{:S(2)}, u32[]{:S(2)}) collective-permute-start(bf16[2,40,896]{2,1,0:T(8,128)(2,1)S(1)} %get-tuple-element.57), channel_id=1, source_target_pairs={{0,192},{64,128},{128,64},{192,0},{1,193},{65,129},{129,65},{193,1... | collective-permute-start | bytes 430088 | tf_op jit(solution)/shard_map/ppermute | solution.py:24
  130.5 20.7 %collective-permute-start.14 = (bf16[192,896]{1,0:T(8,128)(2,1)S(1)}, bf16[192,896]{1,0:T(8,128)(2,1)S(1)}, u32[]{:S(2)}, u32[]{:S(2)}) collective-permute-start(bf16[192,896]{1,0:T(8,128)(2,1)S(1)} %slice.135), channel_id=1, source_target_pairs={{0,1},{1,0},{2,3},{3,2},{4,5},{5,4},{6,7},{7,6},{8,9},{9,8},{10,11... | collective-permute-start | bytes 1032200 | tf_op jit(solution)/shard_map/ppermute | solution.py:24
  131.5 19.0 %collective-permute-start.16 = (bf16[192,896]{1,0:T(8,128)(2,1)S(1)}, bf16[192,896]{1,0:T(8,128)(2,1)S(1)}, u32[]{:S(2)}, u32[]{:S(2)}) collective-permute-start(bf16[192,896]{1,0:T(8,128)(2,1)S(1)} %slice.135), channel_id=1, source_target_pairs={{0,3},{1,2},{2,1},{3,0},{4,7},{5,6},{6,5},{7,4},{8,11},{9,10},{10,... | collective-permute-start | bytes 1032200 | tf_op jit(solution)/shard_map/ppermute | solution.py:24
  133.1 20.2 %collective-permute-start.17 = (bf16[320,896]{1,0:T(8,128)(2,1)S(1)}, bf16[320,896]{1,0:T(8,128)(2,1)S(1)}, u32[]{:S(2)}, u32[]{:S(2)}) collective-permute-start(bf16[320,896]{1,0:T(8,128)(2,1)S(1)} %bitcast.212), channel_id=1, source_target_pairs={{0,4},{4,0},{1,5},{5,1},{2,6},{6,2},{3,7},{7,3},{8,12},{12,8},{9,1... | collective-permute-start | bytes 1720328 | tf_op jit(solution)/shard_map/ppermute | solution.py:24
  134.6 13.7 %collective-permute-start.15 = (bf16[192,896]{1,0:T(8,128)(2,1)S(1)}, bf16[192,896]{1,0:T(8,128)(2,1)S(1)}, u32[]{:S(2)}, u32[]{:S(2)}) collective-permute-start(bf16[192,896]{1,0:T(8,128)(2,1)S(1)} %slice.135), channel_id=1, source_target_pairs={{0,2},{1,3},{2,0},{3,1},{4,6},{5,7},{6,4},{7,5},{8,10},{9,11},{10,... | collective-permute-start | bytes 1032200 | tf_op jit(solution)/shard_map/ppermute | solution.py:24
  148.2 11.2 %collective-permute-start.19 = (bf16[192,896]{1,0:T(8,128)(2,1)S(1)}, bf16[192,896]{1,0:T(8,128)(2,1)S(1)}, u32[]{:S(2)}, u32[]{:S(2)}) collective-permute-start(bf16[192,896]{1,0:T(8,128)(2,1)S(1)} %collective-permute-done.15), channel_id=1, source_target_pairs={{0,4},{4,0},{1,5},{5,1},{2,6},{6,2},{3,7},{7,3},{8,12},{12,8},{9,1... | collective-permute-start | bytes 1032200 | tf_op jit(solution)/shard_map/ppermute | solution.py:24
  150.5 16.3 %collective-permute-start.20 = (bf16[192,896]{1,0:T(8,128)(2,1)S(1)}, bf16[192,896]{1,0:T(8,128)(2,1)S(1)}, u32[]{:S(2)}, u32[]{:S(2)}) collective-permute-start(bf16[192,896]{1,0:T(8,128)(2,1)S(1)} %collective-permute-done.16), channel_id=1, source_target_pairs={{0,4},{4,0},{1,5},{5,1},{2,6},{6,2},{3,7},{7,3},{8,12},{12,8},{9,1... | collective-permute-start | bytes 1032200 | tf_op jit(solution)/shard_map/ppermute | solution.py:24
  151.2 21.1 %collective-permute-start.18 = (bf16[192,896]{1,0:T(8,128)(2,1)S(1)}, bf16[192,896]{1,0:T(8,128)(2,1)S(1)}, u32[]{:S(2)}, u32[]{:S(2)}) collective-permute-start(bf16[192,896]{1,0:T(8,128)(2,1)S(1)} %collective-permute-done.14), channel_id=1, source_target_pairs={{0,4},{4,0},{1,5},{5,1},{2,6},{6,2},{3,7},{7,3},{8,12},{12,8},{9,1... | collective-permute-start | bytes 1032200 | tf_op jit(solution)/shard_map/ppermute | solution.py:24
  153.4 22.3 %collective-permute-start.21 = (bf16[2,128,896]{2,1,0:T(8,128)(2,1)S(1)}, bf16[2,128,896]{2,1,0:T(8,128)(2,1)S(1)}, u32[]{:S(2)}, u32[]{:S(2)}) collective-permute-start(bf16[2,128,896]{2,1,0:T(8,128)(2,1)S(1)} %pad_maximum_fusion.28), channel_id=1, source_target_pairs={{0,1},{1,0},{2,3},{3,2},{4,5},{5,4},{6,7},{7,6},{8,9},{9,8},{10,11... | collective-permute-start | bytes 1376264 | tf_op jit(solution)/shard_map/ppermute | solution.py:24
  153.5 21.6 %collective-permute-start.23 = (bf16[2,128,896]{2,1,0:T(8,128)(2,1)S(1)}, bf16[2,128,896]{2,1,0:T(8,128)(2,1)S(1)}, u32[]{:S(2)}, u32[]{:S(2)}) collective-permute-start(bf16[2,128,896]{2,1,0:T(8,128)(2,1)S(1)} %pad_maximum_fusion.28), channel_id=1, source_target_pairs={{0,3},{1,2},{2,1},{3,0},{4,7},{5,6},{6,5},{7,4},{8,11},{9,10},{10,... | collective-permute-start | bytes 1376264 | tf_op jit(solution)/shard_map/ppermute | solution.py:24
  159.4 16.9 %collective-permute-start.22 = (bf16[2,128,896]{2,1,0:T(8,128)(2,1)S(1)}, bf16[2,128,896]{2,1,0:T(8,128)(2,1)S(1)}, u32[]{:S(2)}, u32[]{:S(2)}) collective-permute-start(bf16[2,128,896]{2,1,0:T(8,128)(2,1)S(1)} %pad_maximum_fusion.28), channel_id=1, source_target_pairs={{0,2},{1,3},{2,0},{3,1},{4,6},{5,7},{6,4},{7,5},{8,10},{9,11},{10,... | collective-permute-start | bytes 1376264 | tf_op jit(solution)/shard_map/ppermute | solution.py:24
  198.8 5.2 %collective-permute-start.24 = (bf16[2,40,896]{2,1,0:T(8,128)(2,1)S(1)}, bf16[2,40,896]{2,1,0:T(8,128)(2,1)S(1)}, u32[]{:S(2)}, u32[]{:S(2)}) collective-permute-start(bf16[2,40,896]{2,1,0:T(8,128)(2,1)S(1)} %bitcast.253), channel_id=1, source_target_pairs={{0,64},{64,0},{128,192},{192,128},{1,65},{65,1},{129,193},{193,129... | collective-permute-start | bytes 430088 | tf_op jit(solution)/shard_map/ppermute | solution.py:24
  198.9 6.2 %collective-permute-start.25 = (bf16[2,40,896]{2,1,0:T(8,128)(2,1)S(1)}, bf16[2,40,896]{2,1,0:T(8,128)(2,1)S(1)}, u32[]{:S(2)}, u32[]{:S(2)}) collective-permute-start(bf16[2,40,896]{2,1,0:T(8,128)(2,1)S(1)} %bitcast.251), channel_id=1, source_target_pairs={{0,128},{64,192},{128,0},{192,64},{1,129},{65,193},{129,1},{193,65... | collective-permute-start | bytes 430088 | tf_op jit(solution)/shard_map/ppermute | solution.py:24
  199.0 10.8 %collective-permute-start.26 = (bf16[2,40,896]{2,1,0:T(8,128)(2,1)S(1)}, bf16[2,40,896]{2,1,0:T(8,128)(2,1)S(1)}, u32[]{:S(2)}, u32[]{:S(2)}) collective-permute-start(bf16[2,40,896]{2,1,0:T(8,128)(2,1)S(1)} %bitcast.249), channel_id=1, source_target_pairs={{0,192},{64,128},{128,64},{192,0},{1,193},{65,129},{129,65},{193,1... | collective-permute-start | bytes 430088 | tf_op jit(solution)/shard_map/ppermute | solution.py:24
  210.0 1.7 collective-permute-start.27
  212.8 20.0 %all-to-all-start.6 = ((bf16[32,4,896]{2,1,0:T(4,128)(2,1)}), bf16[32,4,896]{2,1,0:T(4,128)(2,1)S(1)}, u32[]{:S(2)}, u32[]{:S(2)}) async-start(bf16[32,4,896]{2,1,0:T(4,128)(2,1)} %reshape.377), calls=%async_computation.6 | async-start | bytes 458752 | tf_op jit(solution)/shard_map/all_to_all | solution.py:20
  (24 other events, 224.5 us)
where the time goes:
time: 235 us; the launch traced here: 234 us
  waiting for transfers between devices  101 us (43%)
  starting transfers between devices  63.2 us (27%)
  blocking collectives  30.7 us (13%)
  local copies, waits for them, and re-layouts  17.4 us (7%)
  matrix products  15.2 us (6%)
  other arithmetic  5.5 us (2%)
    ppermute x28, waiting for transfers between devices, swap(): return lax.ppermute(value, axes, [(i, i ^ mask) for i in range(count)])  56.8 us
    all_to_all x5, waiting for transfers between devices, all_to_all(): return lax.all_to_all(value, axes, split_axis=0, concat_axis=0, tiled=True)  44 us
    ppermute x28, starting transfers between devices, swap(): return lax.ppermute(value, axes, [(i, i ^ mask) for i in range(count)])  35.8 us
    all_to_all x2, blocking collectives, all_to_all(): return lax.all_to_all(value, axes, split_axis=0, concat_axis=0, tiled=True)  30.7 us
    all_to_all x5, starting transfers between devices, all_to_all(): return lax.all_to_all(value, axes, split_axis=0, concat_axis=0, tiled=True)  27.4 us
    dot_general x16, matrix products, activate(): pre = pre + jnp.dot(piece, weight, preferred_element_type=jnp.float32)  6.69 us
    dynamic_slice x1, local copies, waits for them, and re-layouts, on_device(): lax.dynamic_slice_in_dim(up_weight, first, share, 0)  5.53 us
  transfers between devices with their start and end apart: 33, of which 24 were waited for; matrix products, arithmetic and copies ran while one was open for 11% of the time, Pallas kernels for 0%

commit v1 on v0

--- a/solution.py
+++ b/solution.py
@@ -127,7 +127,7 @@
     member = lax.axis_index(EXP)
     patch_here = lax.axis_index(PATCH)
 
-    early = hidden_share * 9 // 16
+    early = hidden_share // 2
     down_early = all_to_all(
         down_weight[:early].reshape(early, 8, share).transpose(1, 0, 2), PATCH
     )

time: 235 us -> 245 us (1.043)
  local copies, waits for them, and re-layouts: 17.4 us -> 31 us
  waiting for transfers between devices: 101 us -> 95.4 us
  other arithmetic: 5.5 us -> 7.99 us
    unnamed x53 -> x73, local copies, waits for them, and re-layouts: 3.17 us -> 8.15 us
    all_to_all x5, waiting for transfers between devices: 44 us -> 39.4 us  [all_to_all(): return lax.all_to_all(value, axes, split_axis=0, concat_axis=0, tiled=True)]
    slice x2 -> x1, local copies, waits for them, and re-layouts: 0.37 us -> 3.51 us  [on_device(): down_weight[early:].reshape(hidden_share - early, 8, share)]
    reshape x1, local copies, waits for them, and re-layouts: 1.33 us -> 3.8 us  [on_device(): down_weight[early:].reshape(hidden_share - early, 8, share)]
  transfers between devices with their start and end apart: 33 -> 33, of which waited for: 24 -> 24; matrix products, arithmetic and copies ran while one was open for 11% -> 17% of each run, Pallas kernels for 0% -> 0%
where the time goes in v1:
time: 245 us; the launch traced here: 244 us
  waiting for transfers between devices  95.4 us (39%)
  starting transfers between devices  64.1 us (26%)
  local copies, waits for them, and re-layouts  31 us (13%)
  blocking collectives  30 us (12%)
  matrix products  14.3 us (6%)
  other arithmetic  7.99 us (3%)
    ppermute x28, waiting for transfers between devices, swap(): return lax.ppermute(value, axes, [(i, i ^ mask) for i in range(count)])  56 us
    all_to_all x5, waiting for transfers between devices, all_to_all(): return lax.all_to_all(value, axes, split_axis=0, concat_axis=0, tiled=True)  39.4 us
    ppermute x28, starting transfers between devices, swap(): return lax.ppermute(value, axes, [(i, i ^ mask) for i in range(count)])  35.7 us
    all_to_all x2, blocking collectives, all_to_all(): return lax.all_to_all(value, axes, split_axis=0, concat_axis=0, tiled=True)  30 us
    all_to_all x5, starting transfers between devices, all_to_all(): return lax.all_to_all(value, axes, split_axis=0, concat_axis=0, tiled=True)  28.4 us
    unnamed x73, local copies, waits for them, and re-layouts  8.15 us
    dot_general x16, matrix products, activate(): pre = pre + jnp.dot(piece, weight, preferred_element_type=jnp.float32)  6.7 us
    dynamic_slice x1, local copies, waits for them, and re-layouts, on_device(): lax.dynamic_slice_in_dim(up_weight, first, share, 0)  5.82 us
  transfers between devices with their start and end apart: 33, of which 24 were waited for; matrix products, arithmetic and copies ran while one was open for 17% of the time, Pallas kernels for 0%

profile of v1, /device:TPU:32, one launch (start us, length us, event | category | flops | bytes accessed | tf_op | source)
XLA Modules:
  0.0 243.9 jit_solution(8084536137247911539)
XLA Ops:
  1.8 3.4 %collective-permute-start.1 = (bf16[128,576]{0,1:T(8,128)(2,1)S(1)}, bf16[128,576]{0,1:T(8,128)(2,1)S(1)}, u32[]{:S(2)}, u32[]{:S(2)}) collective-permute-start(bf16[128,576]{0,1:T(8,128)(2,1)S(1)} %get-tuple-element.64), channel_id=1, source_target_pairs={{0,128},{64,192},{128,0},{192,64},{1,129},{65,193},{129,1},{193,65... | collective-permute-start | bytes 442376 | tf_op jit(solution)/shard_map/ppermute | solution.py:24
  6.8 3.5 %fusion.99 = (bf16[128,7168]{1,0:T(8,128)(2,1)S(1)}, bf16[128,7168]{1,0:T(8,128)(2,1)}) fusion(bf16[256,7168]{1,0:T(8,128)(2,1)} %param.28), kind=kLoop, calls=%fused_computation.224 | loop fusion | bytes 7340032 | tf_op jit(solution)/shard_map/slice | solution.py:161
  10.3 3.9 %copy.138 = bf16[128,7168]{0,1:T(8,128)(2,1)} copy(bf16[128,7168]{1,0:T(8,128)(2,1)} %get-tuple-element.50) | data formatting | bytes 3670016
  14.1 3.8 %copy.120 = bf16[128,8,896]{2,0,1:T(8,128)(2,1)} copy(bf16[128,8,896]{0,2,1:T(8,128)(2,1)} %bitcast.198) | data formatting | bytes 3670016 | tf_op jit(solution)/shard_map/reshape | solution.py:132
  17.9 5.5 %all-to-all-start = ((bf16[8,128,896]{2,1,0:T(8,128)(2,1)}), bf16[8,128,896]{2,1,0:T(8,128)(2,1)}, u32[]{:S(2)}, u32[]{:S(2)}) async-start(bf16[8,128,896]{2,1,0:T(8,128)(2,1)} %bitcast.197), calls=%async_computation | async-start | bytes 3670016 | tf_op jit(solution)/shard_map/all_to_all | solution.py:20
  33.4 2.5 %collective-permute-start.5 = (bf16[128,256]{1,0:T(8,128)(2,1)S(1)}, bf16[128,256]{1,0:T(8,128)(2,1)S(1)}, u32[]{:S(2)}, u32[]{:S(2)}) collective-permute-start(bf16[128,256]{1,0:T(8,128)(2,1)S(1)} %copy.114), channel_id=1, source_target_pairs={{0,128},{64,192},{128,0},{192,64},{1,129},{65,193},{129,1},{193,65... | collective-permute-start | bytes 196616 | tf_op jit(solution)/shard_map/ppermute | solution.py:24
  37.1 3.4 %collective-permute-done.5 = bf16[128,256]{1,0:T(8,128)(2,1)S(1)} collective-permute-done((bf16[128,256]{1,0:T(8,128)(2,1)S(1)}, bf16[128,256]{1,0:T(8,128)(2,1)S(1)}, u32[]{:S(2)}, u32[]{:S(2)}) %collective-permute-start.5) | collective-permute-done | bytes 65568 | tf_op jit(solution)/shard_map/ppermute | solution.py:24
  46.2 7.0 %all-to-all-start.1 = ((bf16[16,64,896]{2,1,0:T(8,128)(2,1)}), bf16[16,64,896]{2,1,0:T(8,128)(2,1)}, u32[]{:S(2)}, u32[]{:S(2)}) async-start(bf16[16,64,896]{2,1,0:T(8,128)(2,1)} %bitcast.200), calls=%async_computation.1 | async-start | bytes 3670016 | tf_op jit(solution)/shard_map/all_to_all | solution.py:20
  56.6 3.8 %copy.122 = bf16[128,8,896]{2,0,1:T(8,128)(2,1)} copy(bf16[128,8,896]{0,2,1:T(8,128)(2,1)} %bitcast.199) | data formatting | bytes 3670016 | tf_op jit(solution)/shard_map/reshape | solution.py:161
  61.6 5.9 %collective-permute-start.8 = (bf16[4,7168]{1,0:T(4,128)(2,1)S(1)}, bf16[4,7168]{1,0:T(4,128)(2,1)S(1)}, u32[]{:S(2)}, u32[]{:S(2)}) collective-permute-start(bf16[4,7168]{1,0:T(4,128)(2,1)S(1)} %copy-done.23), channel_id=1, source_target_pairs={{0,16},{16,0},{1,17},{17,1},{2,18},{18,2},{3,19},{19,3},{4,20},{20... | collective-permute-start | bytes 172040 | tf_op jit(solution)/shard_map/ppermute | solution.py:24
  68.4 2.5 %collective-permute-done.8 = bf16[4,7168]{1,0:T(4,128)(2,1)S(1)} collective-permute-done((bf16[4,7168]{1,0:T(4,128)(2,1)S(1)}, bf16[4,7168]{1,0:T(4,128)(2,1)S(1)}, u32[]{:S(2)}, u32[]{:S(2)}) %collective-permute-start.8) | collective-permute-done | bytes 57376 | tf_op jit(solution)/shard_map/ppermute | solution.py:24
  70.9 10.1 %all-to-all-done.1 = bf16[16,64,896]{2,1,0:T(8,128)(2,1)} async-done(((bf16[16,64,896]{2,1,0:T(8,128)(2,1)}), bf16[16,64,896]{2,1,0:T(8,128)(2,1)}, u32[]{:S(2)}, u32[]{:S(2)}) %all-to-all-start.1) | async-done | bytes 1835040 | tf_op jit(solution)/shard_map/all_to_all | solution.py:20
  84.9 7.7 %all-to-all-start.2 = ((bf16[8,2,8,896]{3,2,1,0:T(8,128)(2,1)}), bf16[8,2,8,896]{3,2,1,0:T(8,128)(2,1)S(1)}, u32[]{:S(2)}, u32[]{:S(2)}) async-start(bf16[8,2,8,896]{3,2,1,0:T(8,128)(2,1)} %bitcast.41), calls=%async_computation.2 | async-start | bytes 458752 | tf_op jit(solution)/shard_map/all_to_all | solution.py:20
  92.6 9.7 %all-to-all-done.2 = bf16[8,2,8,896]{3,2,1,0:T(8,128)(2,1)S(1)} async-done(((bf16[8,2,8,896]{3,2,1,0:T(8,128)(2,1)}), bf16[8,2,8,896]{3,2,1,0:T(8,128)(2,1)S(1)}, u32[]{:S(2)}, u32[]{:S(2)}) %all-to-all-start.2) | async-done | bytes 229408 | tf_op jit(solution)/shard_map/all_to_all | solution.py:20
  102.7 11.7 %all_to_all.35 = bf16[16,8,896]{2,1,0:T(8,128)(2,1)S(1)} all-to-all(bf16[16,8,896]{2,1,0:T(8,128)(2,1)S(1)} %bitcast.219), channel_id=1, replica_groups=mesh['zl'=4,'core'=2,'zh'=2,'x2'=2,'x1'=2,'y'=4] {'x2','x1','y'}, dimensions={0} | all-to-all | bytes 458752 | tf_op jit(solution)/shard_map/all_to_all | solution.py:20
  114.8 3.6 %all-to-all-start.4 = ((bf16[8,128,896]{2,1,0:T(8,128)(2,1)}), bf16[8,128,896]{2,1,0:T(8,128)(2,1)S(1)}, u32[]{:S(2)}, u32[]{:S(2)}) async-start(bf16[8,128,896]{2,1,0:T(8,128)(2,1)} %bitcast.30), calls=%async_computation.4 | async-start | bytes 3670016 | tf_op jit(solution)/shard_map/all_to_all | solution.py:20
  123.7 5.8 %constant_dynamic-slice_fusion.10 = (bf16[896,256]{1,0:T(8,128)(2,1)S(1)}, bf16[896,256]{1,0:T(8,128)(2,1)}, bf16[896,256]{1,0:T(8,128)(2,1)}, bf16[896,256]{1,0...) fusion(bf16[7168,256]{1,0:T(8,128)(2,1)} %param.27, ...), kind=kLoop, calls=%fused_computation.162 | loop fusion | bytes 14680096 | tf_op jit(solution)/shard_map/dynamic_slice | solution.py:233
  129.6 3.2 %collective-permute-done.12 = bf16[2,40,896]{2,1,0:T(8,128)(2,1)S(1)} collective-permute-done((bf16[2,40,896]{2,1,0:T(8,128)(2,1)S(1)}, bf16[2,40,896]{2,1,0:T(8,128)(2,1)S(1)}, u32[]{:S(2)}, u32[]{:S(2)}) %collective-permute-start.12) | collective-permute-done | bytes 143392 | tf_op jit(solution)/shard_map/ppermute | solution.py:24
  132.8 3.7 %collective-permute-done.13 = bf16[2,40,896]{2,1,0:T(8,128)(2,1)S(1)} collective-permute-done((bf16[2,40,896]{2,1,0:T(8,128)(2,1)S(1)}, bf16[2,40,896]{2,1,0:T(8,128)(2,1)S(1)}, u32[]{:S(2)}, u32[]{:S(2)}) %collective-permute-start.13) | collective-permute-done | bytes 143392 | tf_op jit(solution)/shard_map/ppermute | solution.py:24
  136.6 4.1 %all-to-all-done.4 = bf16[8,128,896]{2,1,0:T(8,128)(2,1)S(1)} async-done(((bf16[8,128,896]{2,1,0:T(8,128)(2,1)}), bf16[8,128,896]{2,1,0:T(8,128)(2,1)S(1)}, u32[]{:S(2)}, u32[]{:S(2)}) %all-to-all-start.4) | async-done | bytes 1835040 | tf_op jit(solution)/shard_map/all_to_all | solution.py:20
  143.8 2.6 %collective-permute-start.15 = (bf16[192,896]{1,0:T(8,128)(2,1)S(1)}, bf16[192,896]{1,0:T(8,128)(2,1)S(1)}, u32[]{:S(2)}, u32[]{:S(2)}) collective-permute-start(bf16[192,896]{1,0:T(8,128)(2,1)S(1)} %slice.135), channel_id=1, source_target_pairs={{0,2},{1,3},{2,0},{3,1},{4,6},{5,7},{6,4},{7,5},{8,10},{9,11},{10,... | collective-permute-start | bytes 1032200 | tf_op jit(solution)/shard_map/ppermute | solution.py:24
  148.4 9.8 %collective-permute-done.15 = bf16[192,896]{1,0:T(8,128)(2,1)S(1)} collective-permute-done((bf16[192,896]{1,0:T(8,128)(2,1)S(1)}, bf16[192,896]{1,0:T(8,128)(2,1)S(1)}, u32[]{:S(2)}, u32[]{:S(2)}) %collective-permute-start.15) | collective-permute-done | bytes 344096 | tf_op jit(solution)/shard_map/ppermute | solution.py:24
  158.2 2.5 %collective-permute-start.19 = (bf16[192,896]{1,0:T(8,128)(2,1)S(1)}, bf16[192,896]{1,0:T(8,128)(2,1)S(1)}, u32[]{:S(2)}, u32[]{:S(2)}) collective-permute-start(bf16[192,896]{1,0:T(8,128)(2,1)S(1)} %collective-permute-done.15), channel_id=1, source_target_pairs={{0,4},{4,0},{1,5},{5,1},{2,6},{6,2},{3,7},{7,3},{8,12},{12,8},{9,1... | collective-permute-start | bytes 1032200 | tf_op jit(solution)/shard_map/ppermute | solution.py:24
  166.8 2.8 %collective-permute-done.19 = bf16[192,896]{1,0:T(8,128)(2,1)S(1)} collective-permute-done((bf16[192,896]{1,0:T(8,128)(2,1)S(1)}, bf16[192,896]{1,0:T(8,128)(2,1)S(1)}, u32[]{:S(2)}, u32[]{:S(2)}) %collective-permute-start.19) | collective-permute-done | bytes 344096 | tf_op jit(solution)/shard_map/ppermute | solution.py:24
  171.5 5.5 %collective-permute-done.20 = bf16[192,896]{1,0:T(8,128)(2,1)S(1)} collective-permute-done((bf16[192,896]{1,0:T(8,128)(2,1)S(1)}, bf16[192,896]{1,0:T(8,128)(2,1)S(1)}, u32[]{:S(2)}, u32[]{:S(2)}) %collective-permute-start.20) | collective-permute-done | bytes 344096 | tf_op jit(solution)/shard_map/ppermute | solution.py:24
  177.4 5.3 %collective-permute-done.18 = bf16[192,896]{1,0:T(8,128)(2,1)S(1)} collective-permute-done((bf16[192,896]{1,0:T(8,128)(2,1)S(1)}, bf16[192,896]{1,0:T(8,128)(2,1)S(1)}, u32[]{:S(2)}, u32[]{:S(2)}) %collective-permute-start.18) | collective-permute-done | bytes 344096 | tf_op jit(solution)/shard_map/ppermute | solution.py:24
  187.6 18.2 %all_to_all.36 = bf16[8,320,256]{2,1,0:T(8,128)(2,1)S(1)} all-to-all(bf16[8,320,256]{2,1,0:T(8,128)(2,1)S(1)} %broadcast_in_dim.100), channel_id=1, replica_groups=mesh['zl'=4,'core'=2,'zh'=2,'x2'=2,'x1'=2,'y'=4] {'x1','y'}, dimensions={0} | all-to-all | bytes 2621440 | tf_op jit(solution)/shard_map/all_to_all | solution.py:20
  205.8 3.0 %fusion.8 = bf16[320,896]{1,0:T(8,128)(2,1)S(1)} fusion(bf16[8,128,896]{2,1,0:T(8,128)(2,1)S(1)} %all-to-all-done.4, bf16[8,128,896]{2,1,0:T(8,128)(2,1)} %all-to-all-done, bf16[8,320,256]{2,1,0:T(8,128)(2,1)S(1)} %all_to_all.36), kind=kOutput, calls=%fused_computation.9 | convolution fusion | flops 1182031872 | bytes 5554176 | tf_op jit(solution)/shard_map/dot_general | solution.py:249
  210.1 2.5 %collective-permute-start.26 = (bf16[2,40,896]{2,1,0:T(8,128)(2,1)S(1)}, bf16[2,40,896]{2,1,0:T(8,128)(2,1)S(1)}, u32[]{:S(2)}, u32[]{:S(2)}) collective-permute-start(bf16[2,40,896]{2,1,0:T(8,128)(2,1)S(1)} %bitcast.241), channel_id=1, source_target_pairs={{0,192},{64,128},{128,64},{192,0},{1,193},{65,129},{129,65},{193,1... | collective-permute-start | bytes 430088 | tf_op jit(solution)/shard_map/ppermute | solution.py:24
  215.2 4.8 %collective-permute-done.26 = bf16[2,40,896]{2,1,0:T(8,128)(2,1)S(1)} collective-permute-done((bf16[2,40,896]{2,1,0:T(8,128)(2,1)S(1)}, bf16[2,40,896]{2,1,0:T(8,128)(2,1)S(1)}, u32[]{:S(2)}, u32[]{:S(2)}) %collective-permute-start.26) | collective-permute-done | bytes 143392 | tf_op jit(solution)/shard_map/ppermute | solution.py:24
  223.0 4.5 %all-to-all-start.6 = ((bf16[32,4,896]{2,1,0:T(4,128)(2,1)}), bf16[32,4,896]{2,1,0:T(4,128)(2,1)S(1)}, u32[]{:S(2)}, u32[]{:S(2)}) async-start(bf16[32,4,896]{2,1,0:T(4,128)(2,1)} %reshape.377), calls=%async_computation.6 | async-start | bytes 458752 | tf_op jit(solution)/shard_map/all_to_all | solution.py:20
  227.6 15.4 %all-to-all-done.6 = bf16[32,4,896]{2,1,0:T(4,128)(2,1)S(1)} async-done(((bf16[32,4,896]{2,1,0:T(4,128)(2,1)}), bf16[32,4,896]{2,1,0:T(4,128)(2,1)S(1)}, u32[]{:S(2)}, u32[]{:S(2)}) %all-to-all-start.6) | async-done | bytes 229408 | tf_op jit(solution)/shard_map/all_to_all | solution.py:20
  (205 shorter events, 61.1 us)
Async XLA Ops:
  1.8 26.1 %collective-permute-start.1 = (bf16[128,576]{0,1:T(8,128)(2,1)S(1)}, bf16[128,576]{0,1:T(8,128)(2,1)S(1)}, u32[]{:S(2)}, u32[]{:S(2)}) collective-permute-start(bf16[128,576]{0,1:T(8,128)(2,1)S(1)} %get-tuple-element.64), channel_id=1, source_target_pairs={{0,128},{64,192},{128,0},{192,64},{1,129},{65,193},{129,1},{193,65... | collective-permute-start | bytes 442376 | tf_op jit(solution)/shard_map/ppermute | solution.py:24
  5.2 22.7 %collective-permute-start.2 = (bf16[128,576]{0,1:T(8,128)(2,1)S(1)}, bf16[128,576]{0,1:T(8,128)(2,1)S(1)}, u32[]{:S(2)}, u32[]{:S(2)}) collective-permute-start(bf16[128,576]{0,1:T(8,128)(2,1)S(1)} %get-tuple-element.64), channel_id=1, source_target_pairs={{0,192},{64,128},{128,64},{192,0},{1,193},{65,129},{129,65},{193,1... | collective-permute-start | bytes 442376 | tf_op jit(solution)/shard_map/ppermute | solution.py:24
  5.2 22.7 %collective-permute-start = (bf16[128,576]{0,1:T(8,128)(2,1)S(1)}, bf16[128,576]{0,1:T(8,128)(2,1)S(1)}, u32[]{:S(2)}, u32[]{:S(2)}) collective-permute-start(bf16[128,576]{0,1:T(8,128)(2,1)S(1)} %get-tuple-element.64), channel_id=1, source_target_pairs={{0,64},{64,0},{128,192},{192,128},{1,65},{65,1},{129,193},{193,129... | collective-permute-start | bytes 442376 | tf_op jit(solution)/shard_map/ppermute | solution.py:24
  17.9 28.3 %all-to-all-start = ((bf16[8,128,896]{2,1,0:T(8,128)(2,1)}), bf16[8,128,896]{2,1,0:T(8,128)(2,1)}, u32[]{:S(2)}, u32[]{:S(2)}) async-start(bf16[8,128,896]{2,1,0:T(8,128)(2,1)} %bitcast.197), calls=%async_computation | async-start | bytes 3670016 | tf_op jit(solution)/shard_map/all_to_all | solution.py:20
  28.0 2.1 collective-permute-start.3
  32.8 4.4 %collective-permute-start.4 = (bf16[128,256]{1,0:T(8,128)(2,1)S(1)}, bf16[128,256]{1,0:T(8,128)(2,1)S(1)}, u32[]{:S(2)}, u32[]{:S(2)}) collective-permute-start(bf16[128,256]{1,0:T(8,128)(2,1)S(1)} %copy.114), channel_id=1, source_target_pairs={{0,64},{64,0},{128,192},{192,128},{1,65},{65,1},{129,193},{193,129... | collective-permute-start | bytes 196616 | tf_op jit(solution)/shard_map/ppermute | solution.py:24
  33.4 7.2 %collective-permute-start.5 = (bf16[128,256]{1,0:T(8,128)(2,1)S(1)}, bf16[128,256]{1,0:T(8,128)(2,1)S(1)}, u32[]{:S(2)}, u32[]{:S(2)}) collective-permute-start(bf16[128,256]{1,0:T(8,128)(2,1)S(1)} %copy.114), channel_id=1, source_target_pairs={{0,128},{64,192},{128,0},{192,64},{1,129},{65,193},{129,1},{193,65... | collective-permute-start | bytes 196616 | tf_op jit(solution)/shard_map/ppermute | solution.py:24
  35.8 6.6 %collective-permute-start.6 = (bf16[128,256]{1,0:T(8,128)(2,1)S(1)}, bf16[128,256]{1,0:T(8,128)(2,1)S(1)}, u32[]{:S(2)}, u32[]{:S(2)}) collective-permute-start(bf16[128,256]{1,0:T(8,128)(2,1)S(1)} %copy.114), channel_id=1, source_target_pairs={{0,192},{64,128},{128,64},{192,0},{1,193},{65,129},{129,65},{193,1... | collective-permute-start | bytes 196616 | tf_op jit(solution)/shard_map/ppermute | solution.py:24
  42.5 1.6 collective-permute-start.7
  46.2 34.7 %all-to-all-start.1 = ((bf16[16,64,896]{2,1,0:T(8,128)(2,1)}), bf16[16,64,896]{2,1,0:T(8,128)(2,1)}, u32[]{:S(2)}, u32[]{:S(2)}) async-start(bf16[16,64,896]{2,1,0:T(8,128)(2,1)} %bitcast.200), calls=%async_computation.1 | async-start | bytes 3670016 | tf_op jit(solution)/shard_map/all_to_all | solution.py:20
  61.6 9.2 %collective-permute-start.8 = (bf16[4,7168]{1,0:T(4,128)(2,1)S(1)}, bf16[4,7168]{1,0:T(4,128)(2,1)S(1)}, u32[]{:S(2)}, u32[]{:S(2)}) collective-permute-start(bf16[4,7168]{1,0:T(4,128)(2,1)S(1)} %copy-done.23), channel_id=1, source_target_pairs={{0,16},{16,0},{1,17},{17,1},{2,18},{18,2},{3,19},{19,3},{4,20},{20... | collective-permute-start | bytes 172040 | tf_op jit(solution)/shard_map/ppermute | solution.py:24
  84.9 17.4 %all-to-all-start.2 = ((bf16[8,2,8,896]{3,2,1,0:T(8,128)(2,1)}), bf16[8,2,8,896]{3,2,1,0:T(8,128)(2,1)S(1)}, u32[]{:S(2)}, u32[]{:S(2)}) async-start(bf16[8,2,8,896]{3,2,1,0:T(8,128)(2,1)} %bitcast.41), calls=%async_computation.2 | async-start | bytes 458752 | tf_op jit(solution)/shard_map/all_to_all | solution.py:20
  114.8 25.9 %all-to-all-start.4 = ((bf16[8,128,896]{2,1,0:T(8,128)(2,1)}), bf16[8,128,896]{2,1,0:T(8,128)(2,1)S(1)}, u32[]{:S(2)}, u32[]{:S(2)}) async-start(bf16[8,128,896]{2,1,0:T(8,128)(2,1)} %bitcast.30), calls=%async_computation.4 | async-start | bytes 3670016 | tf_op jit(solution)/shard_map/all_to_all | solution.py:20
  118.4 1.7 collective-permute-start.10
  120.2 9.4 %collective-permute-start.11 = (bf16[2,40,896]{2,1,0:T(8,128)(2,1)S(1)}, bf16[2,40,896]{2,1,0:T(8,128)(2,1)S(1)}, u32[]{:S(2)}, u32[]{:S(2)}) collective-permute-start(bf16[2,40,896]{2,1,0:T(8,128)(2,1)S(1)} %get-tuple-element.58), channel_id=1, source_target_pairs={{0,64},{64,0},{128,192},{192,128},{1,65},{65,1},{129,193},{193,129... | collective-permute-start | bytes 430088 | tf_op jit(solution)/shard_map/ppermute | solution.py:24
  120.3 12.5 %collective-permute-start.12 = (bf16[2,40,896]{2,1,0:T(8,128)(2,1)S(1)}, bf16[2,40,896]{2,1,0:T(8,128)(2,1)S(1)}, u32[]{:S(2)}, u32[]{:S(2)}) collective-permute-start(bf16[2,40,896]{2,1,0:T(8,128)(2,1)S(1)} %get-tuple-element.60), channel_id=1, source_target_pairs={{0,128},{64,192},{128,0},{192,64},{1,129},{65,193},{129,1},{193,65... | collective-permute-start | bytes 430088 | tf_op jit(solution)/shard_map/ppermute | solution.py:24
  122.5 14.0 %collective-permute-start.13 = (bf16[2,40,896]{2,1,0:T(8,128)(2,1)S(1)}, bf16[2,40,896]{2,1,0:T(8,128)(2,1)S(1)}, u32[]{:S(2)}, u32[]{:S(2)}) collective-permute-start(bf16[2,40,896]{2,1,0:T(8,128)(2,1)S(1)} %get-tuple-element.59), channel_id=1, source_target_pairs={{0,192},{64,128},{128,64},{192,0},{1,193},{65,129},{129,65},{193,1... | collective-permute-start | bytes 430088 | tf_op jit(solution)/shard_map/ppermute | solution.py:24
  140.7 20.7 %collective-permute-start.14 = (bf16[192,896]{1,0:T(8,128)(2,1)S(1)}, bf16[192,896]{1,0:T(8,128)(2,1)S(1)}, u32[]{:S(2)}, u32[]{:S(2)}) collective-permute-start(bf16[192,896]{1,0:T(8,128)(2,1)S(1)} %slice.135), channel_id=1, source_target_pairs={{0,1},{1,0},{2,3},{3,2},{4,5},{5,4},{6,7},{7,6},{8,9},{9,8},{10,11... | collective-permute-start | bytes 1032200 | tf_op jit(solution)/shard_map/ppermute | solution.py:24
  141.7 19.0 %collective-permute-start.16 = (bf16[192,896]{1,0:T(8,128)(2,1)S(1)}, bf16[192,896]{1,0:T(8,128)(2,1)S(1)}, u32[]{:S(2)}, u32[]{:S(2)}) collective-permute-start(bf16[192,896]{1,0:T(8,128)(2,1)S(1)} %slice.135), channel_id=1, source_target_pairs={{0,3},{1,2},{2,1},{3,0},{4,7},{5,6},{6,5},{7,4},{8,11},{9,10},{10,... | collective-permute-start | bytes 1032200 | tf_op jit(solution)/shard_map/ppermute | solution.py:24
  143.2 20.2 %collective-permute-start.17 = (bf16[320,896]{1,0:T(8,128)(2,1)S(1)}, bf16[320,896]{1,0:T(8,128)(2,1)S(1)}, u32[]{:S(2)}, u32[]{:S(2)}) collective-permute-start(bf16[320,896]{1,0:T(8,128)(2,1)S(1)} %bitcast.204), channel_id=1, source_target_pairs={{0,4},{4,0},{1,5},{5,1},{2,6},{6,2},{3,7},{7,3},{8,12},{12,8},{9,1... | collective-permute-start | bytes 1720328 | tf_op jit(solution)/shard_map/ppermute | solution.py:24
  143.8 14.3 %collective-permute-start.15 = (bf16[192,896]{1,0:T(8,128)(2,1)S(1)}, bf16[192,896]{1,0:T(8,128)(2,1)S(1)}, u32[]{:S(2)}, u32[]{:S(2)}) collective-permute-start(bf16[192,896]{1,0:T(8,128)(2,1)S(1)} %slice.135), channel_id=1, source_target_pairs={{0,2},{1,3},{2,0},{3,1},{4,6},{5,7},{6,4},{7,5},{8,10},{9,11},{10,... | collective-permute-start | bytes 1032200 | tf_op jit(solution)/shard_map/ppermute | solution.py:24
  158.2 11.4 %collective-permute-start.19 = (bf16[192,896]{1,0:T(8,128)(2,1)S(1)}, bf16[192,896]{1,0:T(8,128)(2,1)S(1)}, u32[]{:S(2)}, u32[]{:S(2)}) collective-permute-start(bf16[192,896]{1,0:T(8,128)(2,1)S(1)} %collective-permute-done.15), channel_id=1, source_target_pairs={{0,4},{4,0},{1,5},{5,1},{2,6},{6,2},{3,7},{7,3},{8,12},{12,8},{9,1... | collective-permute-start | bytes 1032200 | tf_op jit(solution)/shard_map/ppermute | solution.py:24
  160.6 16.3 %collective-permute-start.20 = (bf16[192,896]{1,0:T(8,128)(2,1)S(1)}, bf16[192,896]{1,0:T(8,128)(2,1)S(1)}, u32[]{:S(2)}, u32[]{:S(2)}) collective-permute-start(bf16[192,896]{1,0:T(8,128)(2,1)S(1)} %collective-permute-done.16), channel_id=1, source_target_pairs={{0,4},{4,0},{1,5},{5,1},{2,6},{6,2},{3,7},{7,3},{8,12},{12,8},{9,1... | collective-permute-start | bytes 1032200 | tf_op jit(solution)/shard_map/ppermute | solution.py:24
  161.4 21.3 %collective-permute-start.18 = (bf16[192,896]{1,0:T(8,128)(2,1)S(1)}, bf16[192,896]{1,0:T(8,128)(2,1)S(1)}, u32[]{:S(2)}, u32[]{:S(2)}) collective-permute-start(bf16[192,896]{1,0:T(8,128)(2,1)S(1)} %collective-permute-done.14), channel_id=1, source_target_pairs={{0,4},{4,0},{1,5},{5,1},{2,6},{6,2},{3,7},{7,3},{8,12},{12,8},{9,1... | collective-permute-start | bytes 1032200 | tf_op jit(solution)/shard_map/ppermute | solution.py:24
  163.6 22.6 %collective-permute-start.21 = (bf16[2,128,896]{2,1,0:T(8,128)(2,1)S(1)}, bf16[2,128,896]{2,1,0:T(8,128)(2,1)S(1)}, u32[]{:S(2)}, u32[]{:S(2)}) collective-permute-start(bf16[2,128,896]{2,1,0:T(8,128)(2,1)S(1)} %pad_maximum_fusion.28), channel_id=1, source_target_pairs={{0,1},{1,0},{2,3},{3,2},{4,5},{5,4},{6,7},{7,6},{8,9},{9,8},{10,11... | collective-permute-start | bytes 1376264 | tf_op jit(solution)/shard_map/ppermute | solution.py:24
  163.7 21.8 %collective-permute-start.23 = (bf16[2,128,896]{2,1,0:T(8,128)(2,1)S(1)}, bf16[2,128,896]{2,1,0:T(8,128)(2,1)S(1)}, u32[]{:S(2)}, u32[]{:S(2)}) collective-permute-start(bf16[2,128,896]{2,1,0:T(8,128)(2,1)S(1)} %pad_maximum_fusion.28), channel_id=1, source_target_pairs={{0,3},{1,2},{2,1},{3,0},{4,7},{5,6},{6,5},{7,4},{8,11},{9,10},{10,... | collective-permute-start | bytes 1376264 | tf_op jit(solution)/shard_map/ppermute | solution.py:24
  169.6 17.2 %collective-permute-start.22 = (bf16[2,128,896]{2,1,0:T(8,128)(2,1)S(1)}, bf16[2,128,896]{2,1,0:T(8,128)(2,1)S(1)}, u32[]{:S(2)}, u32[]{:S(2)}) collective-permute-start(bf16[2,128,896]{2,1,0:T(8,128)(2,1)S(1)} %pad_maximum_fusion.28), channel_id=1, source_target_pairs={{0,2},{1,3},{2,0},{3,1},{4,6},{5,7},{6,4},{7,5},{8,10},{9,11},{10,... | collective-permute-start | bytes 1376264 | tf_op jit(solution)/shard_map/ppermute | solution.py:24
  209.0 5.2 %collective-permute-start.24 = (bf16[2,40,896]{2,1,0:T(8,128)(2,1)S(1)}, bf16[2,40,896]{2,1,0:T(8,128)(2,1)S(1)}, u32[]{:S(2)}, u32[]{:S(2)}) collective-permute-start(bf16[2,40,896]{2,1,0:T(8,128)(2,1)S(1)} %bitcast.245), channel_id=1, source_target_pairs={{0,64},{64,0},{128,192},{192,128},{1,65},{65,1},{129,193},{193,129... | collective-permute-start | bytes 430088 | tf_op jit(solution)/shard_map/ppermute | solution.py:24
  209.1 6.2 %collective-permute-start.25 = (bf16[2,40,896]{2,1,0:T(8,128)(2,1)S(1)}, bf16[2,40,896]{2,1,0:T(8,128)(2,1)S(1)}, u32[]{:S(2)}, u32[]{:S(2)}) collective-permute-start(bf16[2,40,896]{2,1,0:T(8,128)(2,1)S(1)} %bitcast.243), channel_id=1, source_target_pairs={{0,128},{64,192},{128,0},{192,64},{1,129},{65,193},{129,1},{193,65... | collective-permute-start | bytes 430088 | tf_op jit(solution)/shard_map/ppermute | solution.py:24
  210.1 10.0 %collective-permute-start.26 = (bf16[2,40,896]{2,1,0:T(8,128)(2,1)S(1)}, bf16[2,40,896]{2,1,0:T(8,128)(2,1)S(1)}, u32[]{:S(2)}, u32[]{:S(2)}) collective-permute-start(bf16[2,40,896]{2,1,0:T(8,128)(2,1)S(1)} %bitcast.241), channel_id=1, source_target_pairs={{0,192},{64,128},{128,64},{192,0},{1,193},{65,129},{129,65},{193,1... | collective-permute-start | bytes 430088 | tf_op jit(solution)/shard_map/ppermute | solution.py:24
  220.2 1.7 collective-permute-start.27
  223.0 20.0 %all-to-all-start.6 = ((bf16[32,4,896]{2,1,0:T(4,128)(2,1)}), bf16[32,4,896]{2,1,0:T(4,128)(2,1)S(1)}, u32[]{:S(2)}, u32[]{:S(2)}) async-start(bf16[32,4,896]{2,1,0:T(4,128)(2,1)} %reshape.377), calls=%async_computation.6 | async-start | bytes 458752 | tf_op jit(solution)/shard_map/all_to_all | solution.py:20
  (31 other events, 365.2 us)

commit v2 on v0

--- a/solution.py
+++ b/solution.py
@@ -212,14 +212,10 @@
     down_columns = jnp.concatenate([down_early, down_late], axis=1).reshape(-1, share)
 
     split = 192
-    beside_all = swap(arrived, "x1", 2, 1)
-    first_pieces = [arrived[:split]] + [swap(arrived[:split], "y", 4, mask) for mask in range(1, 4)]
-    first_pieces = (
-        first_pieces
-        + [beside_all[:split]]
-        + [swap(piece, "x1", 2, 1) for piece in first_pieces[1:]]
-    )
-    pair = jnp.stack([arrived[split:], beside_all[split:]])
+    first, last = arrived[:split], arrived[split:]
+    pair = jnp.stack([last, swap(last, "x1", 2, 1)])
+    first_pieces = [first] + [swap(first, "y", 4, mask) for mask in range(1, 4)]
+    first_pieces = first_pieces + [swap(piece, "x1", 2, 1) for piece in first_pieces]
     pairs = [pair] + [swap(pair, "y", 4, mask) for mask in range(1, 4)]
     last_pieces = [both[0] for both in pairs] + [both[1] for both in pairs]
 

time: 235 us -> 236 us (level)
    ppermute x28 -> x29, waiting for transfers between devices: 56.8 us -> 55.3 us  [swap(): return lax.ppermute(value, axes, [(i, i ^ mask) for i in range(count)])]
    ppermute x28 -> x29, starting transfers between devices: 35.8 us -> 36.7 us  [swap(): return lax.ppermute(value, axes, [(i, i ^ mask) for i in range(count)])]
  transfers between devices with their start and end apart: 33 -> 34, of which waited for: 24 -> 23; matrix products, arithmetic and copies ran while one was open for 11% -> 11% of each run, Pallas kernels for 0% -> 0%
where the time goes in v2:
time: 236 us; the launch traced here: 235 us
  waiting for transfers between devices  99.2 us (42%)
  starting transfers between devices  64.2 us (27%)
  blocking collectives  32.4 us (14%)
  local copies, waits for them, and re-layouts  17.4 us (7%)
  matrix products  15.1 us (6%)
  other arithmetic  5.5 us (2%)
    ppermute x29, waiting for transfers between devices, swap(): return lax.ppermute(value, axes, [(i, i ^ mask) for i in range(count)])  55.3 us
    all_to_all x5, waiting for transfers between devices, all_to_all(): return lax.all_to_all(value, axes, split_axis=0, concat_axis=0, tiled=True)  44 us
    ppermute x29, starting transfers between devices, swap(): return lax.ppermute(value, axes, [(i, i ^ mask) for i in range(count)])  36.7 us
    all_to_all x2, blocking collectives, all_to_all(): return lax.all_to_all(value, axes, split_axis=0, concat_axis=0, tiled=True)  32.4 us
    all_to_all x5, starting transfers between devices, all_to_all(): return lax.all_to_all(value, axes, split_axis=0, concat_axis=0, tiled=True)  27.5 us
    dot_general x16, matrix products, activate(): pre = pre + jnp.dot(piece, weight, preferred_element_type=jnp.float32)  6.61 us
    dynamic_slice x1, local copies, waits for them, and re-layouts, on_device(): lax.dynamic_slice_in_dim(up_weight, first, share, 0)  5.55 us
  transfers between devices with their start and end apart: 34, of which 23 were waited for; matrix products, arithmetic and copies ran while one was open for 11% of the time, Pallas kernels for 0%

profile of v2, /device:TPU:32, one launch (start us, length us, event | category | flops | bytes accessed | tf_op | source)
XLA Modules:
  0.0 234.8 jit_solution(13567409508331269924)
XLA Ops:
  1.8 3.4 %collective-permute-start.1 = (bf16[128,576]{0,1:T(8,128)(2,1)S(1)}, bf16[128,576]{0,1:T(8,128)(2,1)S(1)}, u32[]{:S(2)}, u32[]{:S(2)}) collective-permute-start(bf16[128,576]{0,1:T(8,128)(2,1)S(1)} %get-tuple-element.64), channel_id=1, source_target_pairs={{0,128},{64,192},{128,0},{192,64},{1,129},{65,193},{129,1},{193,65... | collective-permute-start | bytes 442376 | tf_op jit(solution)/shard_map/ppermute | solution.py:24
  8.3 5.5 %all-to-all-start = ((bf16[8,144,896]{2,1,0:T(8,128)(2,1)}), bf16[8,144,896]{2,1,0:T(8,128)(2,1)S(1)}, u32[]{:S(2)}, u32[]{:S(2)}) async-start(bf16[8,144,896]{2,1,0:T(8,128)(2,1)} %bitcast.203), calls=%async_computation | async-start | bytes 4128768 | tf_op jit(solution)/shard_map/all_to_all | solution.py:20
  17.7 1.9 collective-permute-done.3
  22.3 3.9 %collective-permute-start.5 = (bf16[128,256]{1,0:T(8,128)(2,1)S(1)}, bf16[128,256]{1,0:T(8,128)(2,1)S(1)}, u32[]{:S(2)}, u32[]{:S(2)}) collective-permute-start(bf16[128,256]{1,0:T(8,128)(2,1)S(1)} %copy.108), channel_id=1, source_target_pairs={{0,128},{64,192},{128,0},{192,64},{1,129},{65,193},{129,1},{193,65... | collective-permute-start | bytes 196616 | tf_op jit(solution)/shard_map/ppermute | solution.py:24
  26.6 3.8 %collective-permute-done.5 = bf16[128,256]{1,0:T(8,128)(2,1)S(1)} collective-permute-done((bf16[128,256]{1,0:T(8,128)(2,1)S(1)}, bf16[128,256]{1,0:T(8,128)(2,1)S(1)}, u32[]{:S(2)}, u32[]{:S(2)}) %collective-permute-start.5) | collective-permute-done | bytes 65568 | tf_op jit(solution)/shard_map/ppermute | solution.py:24
  30.4 1.9 collective-permute-done.6
  34.0 1.9 convolution_convert_fusion
  35.9 3.0 %all-to-all-done = bf16[8,144,896]{2,1,0:T(8,128)(2,1)S(1)} async-done(((bf16[8,144,896]{2,1,0:T(8,128)(2,1)}), bf16[8,144,896]{2,1,0:T(8,128)(2,1)S(1)}, u32[]{:S(2)}, u32[]{:S(2)}) %all-to-all-start) | async-done | bytes 2064416 | tf_op jit(solution)/shard_map/all_to_all | solution.py:20
  40.2 5.5 %all-to-all-start.1 = ((bf16[16,64,896]{2,1,0:T(8,128)(2,1)}), bf16[16,64,896]{2,1,0:T(8,128)(2,1)}, u32[]{:S(2)}, u32[]{:S(2)}) async-start(bf16[16,64,896]{2,1,0:T(8,128)(2,1)} %bitcast.27), calls=%async_computation.1 | async-start | bytes 3670016 | tf_op jit(solution)/shard_map/all_to_all | solution.py:20
  49.8 5.6 %collective-permute-start.8 = (bf16[4,7168]{1,0:T(4,128)(2,1)S(1)}, bf16[4,7168]{1,0:T(4,128)(2,1)S(1)}, u32[]{:S(2)}, u32[]{:S(2)}) collective-permute-start(bf16[4,7168]{1,0:T(4,128)(2,1)S(1)} %copy-done.17), channel_id=1, source_target_pairs={{0,16},{16,0},{1,17},{17,1},{2,18},{18,2},{3,19},{19,3},{4,20},{20... | collective-permute-start | bytes 172040 | tf_op jit(solution)/shard_map/ppermute | solution.py:24
  55.6 2.4 %collective-permute-done.8 = bf16[4,7168]{1,0:T(4,128)(2,1)S(1)} collective-permute-done((bf16[4,7168]{1,0:T(4,128)(2,1)S(1)}, bf16[4,7168]{1,0:T(4,128)(2,1)S(1)}, u32[]{:S(2)}, u32[]{:S(2)}) %collective-permute-start.8) | collective-permute-done | bytes 57376 | tf_op jit(solution)/shard_map/ppermute | solution.py:24
  58.0 14.3 %all-to-all-done.1 = bf16[16,64,896]{2,1,0:T(8,128)(2,1)} async-done(((bf16[16,64,896]{2,1,0:T(8,128)(2,1)}), bf16[16,64,896]{2,1,0:T(8,128)(2,1)}, u32[]{:S(2)}, u32[]{:S(2)}) %all-to-all-start.1) | async-done | bytes 1835040 | tf_op jit(solution)/shard_map/all_to_all | solution.py:20
  72.3 1.8 reduce_sum.60
  76.2 7.4 %all-to-all-start.2 = ((bf16[8,2,8,896]{3,2,1,0:T(8,128)(2,1)}), bf16[8,2,8,896]{3,2,1,0:T(8,128)(2,1)S(1)}, u32[]{:S(2)}, u32[]{:S(2)}) async-start(bf16[8,2,8,896]{3,2,1,0:T(8,128)(2,1)} %bitcast.39), calls=%async_computation.2 | async-start | bytes 458752 | tf_op jit(solution)/shard_map/all_to_all | solution.py:20
  83.7 9.7 %all-to-all-done.2 = bf16[8,2,8,896]{3,2,1,0:T(8,128)(2,1)S(1)} async-done(((bf16[8,2,8,896]{3,2,1,0:T(8,128)(2,1)}), bf16[8,2,8,896]{3,2,1,0:T(8,128)(2,1)S(1)}, u32[]{:S(2)}, u32[]{:S(2)}) %all-to-all-start.2) | async-done | bytes 229408 | tf_op jit(solution)/shard_map/all_to_all | solution.py:20
  93.8 12.1 %all_to_all.35 = bf16[16,8,896]{2,1,0:T(8,128)(2,1)S(1)} all-to-all(bf16[16,8,896]{2,1,0:T(8,128)(2,1)S(1)} %bitcast.227), channel_id=1, replica_groups=mesh['zl'=4,'core'=2,'zh'=2,'x2'=2,'x1'=2,'y'=4] {'x2','x1','y'}, dimensions={0} | all-to-all | bytes 458752 | tf_op jit(solution)/shard_map/all_to_all | solution.py:20
  106.2 4.3 %all-to-all-start.4 = ((bf16[8,112,896]{2,1,0:T(8,128)(2,1)}), bf16[8,112,896]{2,1,0:T(8,128)(2,1)}, u32[]{:S(2)}, u32[]{:S(2)}) async-start(bf16[8,112,896]{2,1,0:T(8,128)(2,1)} %bitcast.205), calls=%async_computation.4 | async-start | bytes 3211264 | tf_op jit(solution)/shard_map/all_to_all | solution.py:20
  112.6 2.2 collective-permute-start.12
  116.1 5.5 %constant_dynamic-slice_fusion.10 = (bf16[896,256]{1,0:T(8,128)(2,1)S(1)}, bf16[896,256]{1,0:T(8,128)(2,1)S(1)}, bf16[896,256]{1,0:T(8,128)(2,1)}, bf16[896,256]...) fusion(bf16[7168,256]{1,0:T(8,128)(2,1)} %param.27, ...), kind=kLoop, calls=%fused_computation.159 | loop fusion | bytes 14680096 | tf_op jit(solution)/shard_map/dynamic_slice | solution.py:229
  121.6 3.5 %collective-permute-done.12 = bf16[2,40,896]{2,1,0:T(8,128)(2,1)S(1)} collective-permute-done((bf16[2,40,896]{2,1,0:T(8,128)(2,1)S(1)}, bf16[2,40,896]{2,1,0:T(8,128)(2,1)S(1)}, u32[]{:S(2)}, u32[]{:S(2)}) %collective-permute-start.12) | collective-permute-done | bytes 143392 | tf_op jit(solution)/shard_map/ppermute | solution.py:24
  125.1 3.7 %collective-permute-done.13 = bf16[2,40,896]{2,1,0:T(8,128)(2,1)S(1)} collective-permute-done((bf16[2,40,896]{2,1,0:T(8,128)(2,1)S(1)}, bf16[2,40,896]{2,1,0:T(8,128)(2,1)S(1)}, u32[]{:S(2)}, u32[]{:S(2)}) %collective-permute-start.13) | collective-permute-done | bytes 143392 | tf_op jit(solution)/shard_map/ppermute | solution.py:24
  138.7 7.8 %collective-permute-done.21 = bf16[128,896]{1,0:T(8,128)(2,1)S(1)} collective-permute-done((bf16[128,896]{1,0:T(8,128)(2,1)S(1)}, bf16[128,896]{1,0:T(8,128)(2,1)S(1)}, u32[]{:S(2)}, u32[]{:S(2)}) %collective-permute-start.21) | collective-permute-done | bytes 229408 | tf_op jit(solution)/shard_map/ppermute | solution.py:24
  148.0 1.8 collective-permute-start.24
  154.9 7.8 %collective-permute-done.19 = bf16[192,896]{1,0:T(8,128)(2,1)S(1)} collective-permute-done((bf16[192,896]{1,0:T(8,128)(2,1)S(1)}, bf16[192,896]{1,0:T(8,128)(2,1)S(1)}, u32[]{:S(2)}, u32[]{:S(2)}) %collective-permute-start.19) | collective-permute-done | bytes 344096 | tf_op jit(solution)/shard_map/ppermute | solution.py:24
  164.8 5.3 %collective-permute-done.20 = bf16[192,896]{1,0:T(8,128)(2,1)S(1)} collective-permute-done((bf16[192,896]{1,0:T(8,128)(2,1)S(1)}, bf16[192,896]{1,0:T(8,128)(2,1)S(1)}, u32[]{:S(2)}, u32[]{:S(2)}) %collective-permute-start.20) | collective-permute-done | bytes 344096 | tf_op jit(solution)/shard_map/ppermute | solution.py:24
  170.4 3.5 %collective-permute-done.18 = bf16[192,896]{1,0:T(8,128)(2,1)S(1)} collective-permute-done((bf16[192,896]{1,0:T(8,128)(2,1)S(1)}, bf16[192,896]{1,0:T(8,128)(2,1)S(1)}, u32[]{:S(2)}, u32[]{:S(2)}) %collective-permute-start.18) | collective-permute-done | bytes 344096 | tf_op jit(solution)/shard_map/ppermute | solution.py:24
  176.6 20.3 %all_to_all.36 = bf16[8,320,256]{2,1,0:T(8,128)(2,1)S(1)} all-to-all(bf16[8,320,256]{2,1,0:T(8,128)(2,1)S(1)} %broadcast_in_dim.100), channel_id=1, replica_groups=mesh['zl'=4,'core'=2,'zh'=2,'x2'=2,'x1'=2,'y'=4] {'x1','y'}, dimensions={0} | all-to-all | bytes 2621440 | tf_op jit(solution)/shard_map/all_to_all | solution.py:20
  196.9 2.9 %fusion.8 = bf16[320,896]{1,0:T(8,128)(2,1)S(1)} fusion(bf16[8,112,896]{2,1,0:T(8,128)(2,1)} %all-to-all-done.4, bf16[8,144,896]{2,1,0:T(8,128)(2,1)S(1)} %copy-done.2, bf16[8,320,256]{2,1,0:T(8,128)(2,1)S(1)} %all_to_all.36), kind=kOutput, calls=%fused_computation.11 | convolution fusion | flops 1182031872 | bytes 5554176 | tf_op jit(solution)/shard_map/dot_general | solution.py:245
  200.1 3.4 %collective-permute-start.27 = (bf16[2,40,896]{2,1,0:T(8,128)(2,1)S(1)}, bf16[2,40,896]{2,1,0:T(8,128)(2,1)S(1)}, u32[]{:S(2)}, u32[]{:S(2)}) collective-permute-start(bf16[2,40,896]{2,1,0:T(8,128)(2,1)S(1)} %bitcast.250), channel_id=1, source_target_pairs={{0,192},{64,128},{128,64},{192,0},{1,193},{65,129},{129,65},{193,1... | collective-permute-start | bytes 430088 | tf_op jit(solution)/shard_map/ppermute | solution.py:24
  206.2 4.7 %collective-permute-done.27 = bf16[2,40,896]{2,1,0:T(8,128)(2,1)S(1)} collective-permute-done((bf16[2,40,896]{2,1,0:T(8,128)(2,1)S(1)}, bf16[2,40,896]{2,1,0:T(8,128)(2,1)S(1)}, u32[]{:S(2)}, u32[]{:S(2)}) %collective-permute-start.27) | collective-permute-done | bytes 143392 | tf_op jit(solution)/shard_map/ppermute | solution.py:24
  213.8 4.7 %all-to-all-start.6 = ((bf16[32,4,896]{2,1,0:T(4,128)(2,1)}), bf16[32,4,896]{2,1,0:T(4,128)(2,1)S(1)}, u32[]{:S(2)}, u32[]{:S(2)}) async-start(bf16[32,4,896]{2,1,0:T(4,128)(2,1)} %reshape.377), calls=%async_computation.6 | async-start | bytes 458752 | tf_op jit(solution)/shard_map/all_to_all | solution.py:20
  218.5 15.4 %all-to-all-done.6 = bf16[32,4,896]{2,1,0:T(4,128)(2,1)S(1)} async-done(((bf16[32,4,896]{2,1,0:T(4,128)(2,1)}), bf16[32,4,896]{2,1,0:T(4,128)(2,1)S(1)}, u32[]{:S(2)}, u32[]{:S(2)}) %all-to-all-start.6) | async-done | bytes 229408 | tf_op jit(solution)/shard_map/all_to_all | solution.py:20
  (189 shorter events, 52.8 us)
Async XLA Ops:
  1.8 14.9 %collective-permute-start.1 = (bf16[128,576]{0,1:T(8,128)(2,1)S(1)}, bf16[128,576]{0,1:T(8,128)(2,1)S(1)}, u32[]{:S(2)}, u32[]{:S(2)}) collective-permute-start(bf16[128,576]{0,1:T(8,128)(2,1)S(1)} %get-tuple-element.64), channel_id=1, source_target_pairs={{0,128},{64,192},{128,0},{192,64},{1,129},{65,193},{129,1},{193,65... | collective-permute-start | bytes 442376 | tf_op jit(solution)/shard_map/ppermute | solution.py:24
  5.2 12.2 %collective-permute-start.2 = (bf16[128,576]{0,1:T(8,128)(2,1)S(1)}, bf16[128,576]{0,1:T(8,128)(2,1)S(1)}, u32[]{:S(2)}, u32[]{:S(2)}) collective-permute-start(bf16[128,576]{0,1:T(8,128)(2,1)S(1)} %get-tuple-element.64), channel_id=1, source_target_pairs={{0,192},{64,128},{128,64},{192,0},{1,193},{65,129},{129,65},{193,1... | collective-permute-start | bytes 442376 | tf_op jit(solution)/shard_map/ppermute | solution.py:24
  5.2 12.1 %collective-permute-start = (bf16[128,576]{0,1:T(8,128)(2,1)S(1)}, bf16[128,576]{0,1:T(8,128)(2,1)S(1)}, u32[]{:S(2)}, u32[]{:S(2)}) collective-permute-start(bf16[128,576]{0,1:T(8,128)(2,1)S(1)} %get-tuple-element.64), channel_id=1, source_target_pairs={{0,64},{64,0},{128,192},{192,128},{1,65},{65,1},{129,193},{193,129... | collective-permute-start | bytes 442376 | tf_op jit(solution)/shard_map/ppermute | solution.py:24
  8.3 30.7 %all-to-all-start = ((bf16[8,144,896]{2,1,0:T(8,128)(2,1)}), bf16[8,144,896]{2,1,0:T(8,128)(2,1)S(1)}, u32[]{:S(2)}, u32[]{:S(2)}) async-start(bf16[8,144,896]{2,1,0:T(8,128)(2,1)} %bitcast.203), calls=%async_computation | async-start | bytes 4128768 | tf_op jit(solution)/shard_map/all_to_all | solution.py:20
  17.5 2.1 collective-permute-start.3
  22.2 4.4 %collective-permute-start.4 = (bf16[128,256]{1,0:T(8,128)(2,1)S(1)}, bf16[128,256]{1,0:T(8,128)(2,1)S(1)}, u32[]{:S(2)}, u32[]{:S(2)}) collective-permute-start(bf16[128,256]{1,0:T(8,128)(2,1)S(1)} %copy.108), channel_id=1, source_target_pairs={{0,64},{64,0},{128,192},{192,128},{1,65},{65,1},{129,193},{193,129... | collective-permute-start | bytes 196616 | tf_op jit(solution)/shard_map/ppermute | solution.py:24
  22.3 8.1 %collective-permute-start.5 = (bf16[128,256]{1,0:T(8,128)(2,1)S(1)}, bf16[128,256]{1,0:T(8,128)(2,1)S(1)}, u32[]{:S(2)}, u32[]{:S(2)}) collective-permute-start(bf16[128,256]{1,0:T(8,128)(2,1)S(1)} %copy.108), channel_id=1, source_target_pairs={{0,128},{64,192},{128,0},{192,64},{1,129},{65,193},{129,1},{193,65... | collective-permute-start | bytes 196616 | tf_op jit(solution)/shard_map/ppermute | solution.py:24
  26.2 6.0 %collective-permute-start.6 = (bf16[128,256]{1,0:T(8,128)(2,1)S(1)}, bf16[128,256]{1,0:T(8,128)(2,1)S(1)}, u32[]{:S(2)}, u32[]{:S(2)}) collective-permute-start(bf16[128,256]{1,0:T(8,128)(2,1)S(1)} %copy.108), channel_id=1, source_target_pairs={{0,192},{64,128},{128,64},{192,0},{1,193},{65,129},{129,65},{193,1... | collective-permute-start | bytes 196616 | tf_op jit(solution)/shard_map/ppermute | solution.py:24
  40.2 32.1 %all-to-all-start.1 = ((bf16[16,64,896]{2,1,0:T(8,128)(2,1)}), bf16[16,64,896]{2,1,0:T(8,128)(2,1)}, u32[]{:S(2)}, u32[]{:S(2)}) async-start(bf16[16,64,896]{2,1,0:T(8,128)(2,1)} %bitcast.27), calls=%async_computation.1 | async-start | bytes 3670016 | tf_op jit(solution)/shard_map/all_to_all | solution.py:20
  49.8 8.2 %collective-permute-start.8 = (bf16[4,7168]{1,0:T(4,128)(2,1)S(1)}, bf16[4,7168]{1,0:T(4,128)(2,1)S(1)}, u32[]{:S(2)}, u32[]{:S(2)}) collective-permute-start(bf16[4,7168]{1,0:T(4,128)(2,1)S(1)} %copy-done.17), channel_id=1, source_target_pairs={{0,16},{16,0},{1,17},{17,1},{2,18},{18,2},{3,19},{19,3},{4,20},{20... | collective-permute-start | bytes 172040 | tf_op jit(solution)/shard_map/ppermute | solution.py:24
  76.2 17.2 %all-to-all-start.2 = ((bf16[8,2,8,896]{3,2,1,0:T(8,128)(2,1)}), bf16[8,2,8,896]{3,2,1,0:T(8,128)(2,1)S(1)}, u32[]{:S(2)}, u32[]{:S(2)}) async-start(bf16[8,2,8,896]{3,2,1,0:T(8,128)(2,1)} %bitcast.39), calls=%async_computation.2 | async-start | bytes 458752 | tf_op jit(solution)/shard_map/all_to_all | solution.py:20
  106.2 24.2 %all-to-all-start.4 = ((bf16[8,112,896]{2,1,0:T(8,128)(2,1)}), bf16[8,112,896]{2,1,0:T(8,128)(2,1)}, u32[]{:S(2)}, u32[]{:S(2)}) async-start(bf16[8,112,896]{2,1,0:T(8,128)(2,1)} %bitcast.205), calls=%async_computation.4 | async-start | bytes 3211264 | tf_op jit(solution)/shard_map/all_to_all | solution.py:20
  110.6 1.8 collective-permute-start.10
  112.5 9.1 %collective-permute-start.11 = (bf16[2,40,896]{2,1,0:T(8,128)(2,1)S(1)}, bf16[2,40,896]{2,1,0:T(8,128)(2,1)S(1)}, u32[]{:S(2)}, u32[]{:S(2)}) collective-permute-start(bf16[2,40,896]{2,1,0:T(8,128)(2,1)S(1)} %get-tuple-element.58), channel_id=1, source_target_pairs={{0,64},{64,0},{128,192},{192,128},{1,65},{65,1},{129,193},{193,129... | collective-permute-start | bytes 430088 | tf_op jit(solution)/shard_map/ppermute | solution.py:24
  112.6 12.5 %collective-permute-start.12 = (bf16[2,40,896]{2,1,0:T(8,128)(2,1)S(1)}, bf16[2,40,896]{2,1,0:T(8,128)(2,1)S(1)}, u32[]{:S(2)}, u32[]{:S(2)}) collective-permute-start(bf16[2,40,896]{2,1,0:T(8,128)(2,1)S(1)} %get-tuple-element.60), channel_id=1, source_target_pairs={{0,128},{64,192},{128,0},{192,64},{1,129},{65,193},{129,1},{193,65... | collective-permute-start | bytes 430088 | tf_op jit(solution)/shard_map/ppermute | solution.py:24
  114.8 14.0 %collective-permute-start.13 = (bf16[2,40,896]{2,1,0:T(8,128)(2,1)S(1)}, bf16[2,40,896]{2,1,0:T(8,128)(2,1)S(1)}, u32[]{:S(2)}, u32[]{:S(2)}) collective-permute-start(bf16[2,40,896]{2,1,0:T(8,128)(2,1)S(1)} %get-tuple-element.59), channel_id=1, source_target_pairs={{0,192},{64,128},{128,64},{192,0},{1,193},{65,129},{129,65},{193,1... | collective-permute-start | bytes 430088 | tf_op jit(solution)/shard_map/ppermute | solution.py:24
  130.5 19.7 %collective-permute-start.14 = (bf16[192,896]{1,0:T(8,128)(2,1)S(1)}, bf16[192,896]{1,0:T(8,128)(2,1)S(1)}, u32[]{:S(2)}, u32[]{:S(2)}) collective-permute-start(bf16[192,896]{1,0:T(8,128)(2,1)S(1)} %slice.126), channel_id=1, source_target_pairs={{0,1},{1,0},{2,3},{3,2},{4,5},{5,4},{6,7},{7,6},{8,9},{9,8},{10,11... | collective-permute-start | bytes 1032200 | tf_op jit(solution)/shard_map/ppermute | solution.py:24
  131.5 21.9 %collective-permute-start.16 = (bf16[192,896]{1,0:T(8,128)(2,1)S(1)}, bf16[192,896]{1,0:T(8,128)(2,1)S(1)}, u32[]{:S(2)}, u32[]{:S(2)}) collective-permute-start(bf16[192,896]{1,0:T(8,128)(2,1)S(1)} %slice.126), channel_id=1, source_target_pairs={{0,3},{1,2},{2,1},{3,0},{4,7},{5,6},{6,5},{7,4},{8,11},{9,10},{10,... | collective-permute-start | bytes 1032200 | tf_op jit(solution)/shard_map/ppermute | solution.py:24
  133.1 15.0 %collective-permute-start.17 = (bf16[192,896]{1,0:T(8,128)(2,1)S(1)}, bf16[192,896]{1,0:T(8,128)(2,1)S(1)}, u32[]{:S(2)}, u32[]{:S(2)}) collective-permute-start(bf16[192,896]{1,0:T(8,128)(2,1)S(1)} %slice.126), channel_id=1, source_target_pairs={{0,4},{4,0},{1,5},{5,1},{2,6},{6,2},{3,7},{7,3},{8,12},{12,8},{9,1... | collective-permute-start | bytes 1032200 | tf_op jit(solution)/shard_map/ppermute | solution.py:24
  134.5 17.1 %collective-permute-start.15 = (bf16[192,896]{1,0:T(8,128)(2,1)S(1)}, bf16[192,896]{1,0:T(8,128)(2,1)S(1)}, u32[]{:S(2)}, u32[]{:S(2)}) collective-permute-start(bf16[192,896]{1,0:T(8,128)(2,1)S(1)} %slice.126), channel_id=1, source_target_pairs={{0,2},{1,3},{2,0},{3,1},{4,6},{5,7},{6,4},{7,5},{8,10},{9,11},{10,... | collective-permute-start | bytes 1032200 | tf_op jit(solution)/shard_map/ppermute | solution.py:24
  136.2 10.3 %collective-permute-start.21 = (bf16[128,896]{1,0:T(8,128)(2,1)S(1)}, bf16[128,896]{1,0:T(8,128)(2,1)S(1)}, u32[]{:S(2)}, u32[]{:S(2)}) collective-permute-start(bf16[128,896]{1,0:T(8,128)(2,1)S(1)} %get-tuple-element.56), channel_id=1, source_target_pairs={{0,4},{4,0},{1,5},{5,1},{2,6},{6,2},{3,7},{7,3},{8,12},{12,8},{9,1... | collective-permute-start | bytes 688136 | tf_op jit(solution)/shard_map/ppermute | solution.py:24
  146.6 28.5 %collective-permute-start.22 = (bf16[2,128,896]{2,1,0:T(8,128)(2,1)S(1)}, bf16[2,128,896]{2,1,0:T(8,128)(2,1)S(1)}, u32[]{:S(2)}, u32[]{:S(2)}) collective-permute-start(bf16[2,128,896]{2,1,0:T(8,128)(2,1)S(1)} %pad_maximum_fusion.28), channel_id=1, source_target_pairs={{0,1},{1,0},{2,3},{3,2},{4,5},{5,4},{6,7},{7,6},{8,9},{9,8},{10,11... | collective-permute-start | bytes 1376264 | tf_op jit(solution)/shard_map/ppermute | solution.py:24
  148.0 26.4 %collective-permute-start.24 = (bf16[2,128,896]{2,1,0:T(8,128)(2,1)S(1)}, bf16[2,128,896]{2,1,0:T(8,128)(2,1)S(1)}, u32[]{:S(2)}, u32[]{:S(2)}) collective-permute-start(bf16[2,128,896]{2,1,0:T(8,128)(2,1)S(1)} %pad_maximum_fusion.28), channel_id=1, source_target_pairs={{0,3},{1,2},{2,1},{3,0},{4,7},{5,6},{6,5},{7,4},{8,11},{9,10},{10,... | collective-permute-start | bytes 1376264 | tf_op jit(solution)/shard_map/ppermute | solution.py:24
  150.2 25.5 %collective-permute-start.23 = (bf16[2,128,896]{2,1,0:T(8,128)(2,1)S(1)}, bf16[2,128,896]{2,1,0:T(8,128)(2,1)S(1)}, u32[]{:S(2)}, u32[]{:S(2)}) collective-permute-start(bf16[2,128,896]{2,1,0:T(8,128)(2,1)S(1)} %pad_maximum_fusion.28), channel_id=1, source_target_pairs={{0,2},{1,3},{2,0},{3,1},{4,6},{5,7},{6,4},{7,5},{8,10},{9,11},{10,... | collective-permute-start | bytes 1376264 | tf_op jit(solution)/shard_map/ppermute | solution.py:24
  151.7 11.0 %collective-permute-start.19 = (bf16[192,896]{1,0:T(8,128)(2,1)S(1)}, bf16[192,896]{1,0:T(8,128)(2,1)S(1)}, u32[]{:S(2)}, u32[]{:S(2)}) collective-permute-start(bf16[192,896]{1,0:T(8,128)(2,1)S(1)} %collective-permute-done.15), channel_id=1, source_target_pairs={{0,4},{4,0},{1,5},{5,1},{2,6},{6,2},{3,7},{7,3},{8,12},{12,8},{9,1... | collective-permute-start | bytes 1032200 | tf_op jit(solution)/shard_map/ppermute | solution.py:24
  153.4 16.7 %collective-permute-start.20 = (bf16[192,896]{1,0:T(8,128)(2,1)S(1)}, bf16[192,896]{1,0:T(8,128)(2,1)S(1)}, u32[]{:S(2)}, u32[]{:S(2)}) collective-permute-start(bf16[192,896]{1,0:T(8,128)(2,1)S(1)} %collective-permute-done.16), channel_id=1, source_target_pairs={{0,4},{4,0},{1,5},{5,1},{2,6},{6,2},{3,7},{7,3},{8,12},{12,8},{9,1... | collective-permute-start | bytes 1032200 | tf_op jit(solution)/shard_map/ppermute | solution.py:24
  162.7 11.3 %collective-permute-start.18 = (bf16[192,896]{1,0:T(8,128)(2,1)S(1)}, bf16[192,896]{1,0:T(8,128)(2,1)S(1)}, u32[]{:S(2)}, u32[]{:S(2)}) collective-permute-start(bf16[192,896]{1,0:T(8,128)(2,1)S(1)} %collective-permute-done.14), channel_id=1, source_target_pairs={{0,4},{4,0},{1,5},{5,1},{2,6},{6,2},{3,7},{7,3},{8,12},{12,8},{9,1... | collective-permute-start | bytes 1032200 | tf_op jit(solution)/shard_map/ppermute | solution.py:24
  199.9 5.2 %collective-permute-start.25 = (bf16[2,40,896]{2,1,0:T(8,128)(2,1)S(1)}, bf16[2,40,896]{2,1,0:T(8,128)(2,1)S(1)}, u32[]{:S(2)}, u32[]{:S(2)}) collective-permute-start(bf16[2,40,896]{2,1,0:T(8,128)(2,1)S(1)} %bitcast.254), channel_id=1, source_target_pairs={{0,64},{64,0},{128,192},{192,128},{1,65},{65,1},{129,193},{193,129... | collective-permute-start | bytes 430088 | tf_op jit(solution)/shard_map/ppermute | solution.py:24
  200.0 6.2 %collective-permute-start.26 = (bf16[2,40,896]{2,1,0:T(8,128)(2,1)S(1)}, bf16[2,40,896]{2,1,0:T(8,128)(2,1)S(1)}, u32[]{:S(2)}, u32[]{:S(2)}) collective-permute-start(bf16[2,40,896]{2,1,0:T(8,128)(2,1)S(1)} %bitcast.252), channel_id=1, source_target_pairs={{0,128},{64,192},{128,0},{192,64},{1,129},{65,193},{129,1},{193,65... | collective-permute-start | bytes 430088 | tf_op jit(solution)/shard_map/ppermute | solution.py:24
  200.1 10.7 %collective-permute-start.27 = (bf16[2,40,896]{2,1,0:T(8,128)(2,1)S(1)}, bf16[2,40,896]{2,1,0:T(8,128)(2,1)S(1)}, u32[]{:S(2)}, u32[]{:S(2)}) collective-permute-start(bf16[2,40,896]{2,1,0:T(8,128)(2,1)S(1)} %bitcast.250), channel_id=1, source_target_pairs={{0,192},{64,128},{128,64},{192,0},{1,193},{65,129},{129,65},{193,1... | collective-permute-start | bytes 430088 | tf_op jit(solution)/shard_map/ppermute | solution.py:24
  211.0 1.7 collective-permute-start.28
  213.8 20.1 %all-to-all-start.6 = ((bf16[32,4,896]{2,1,0:T(4,128)(2,1)}), bf16[32,4,896]{2,1,0:T(4,128)(2,1)S(1)}, u32[]{:S(2)}, u32[]{:S(2)}) async-start(bf16[32,4,896]{2,1,0:T(4,128)(2,1)} %reshape.377), calls=%async_computation.6 | async-start | bytes 458752 | tf_op jit(solution)/shard_map/all_to_all | solution.py:20
  (25 other events, 223.8 us)
